TPU v7x, 32 devices: a whole 2x2x4 slice. The times are simulated.
32 devices in a mesh: pair: 8 (over z, x), virt: 4 (over y, core).
Axes of the slice: x: 2, y: 2, z: 4, core: 2. Of those that a mesh axis runs over, the one named last changes fastest.
Arguments:
- amplitudes: bfloat16 [16, 4, 8, 128], P('pair', None, 'virt'), may hold values from -6 to 6
- kept_groups: int32 [16, 4], P('pair'), may hold values from 0 to 7, all different within a row; in each aligned block of 2 rows (0 to 1, 2 to 3, ...) at most 2 rows name the same one
- tile_mask: int32 [16, 4, 2], P('pair'), may hold values 0 or 1
- owner_table: int32 [8], replicated, may hold values from 0 to 7, each once
- integrals: bfloat16 [1024, 1024], P('pair', 'virt'), may hold values from -0.25 to 0.25
- residual_in: bfloat16 [128, 1024], P('pair', 'virt'), may hold values from -6 to 6
- pair_energy: float32 [128], P('pair'), may hold values from -3 to -1
- virt_energy: float32 [1024], P('virt'), may hold values from 0.5 to 3
Outputs:
- update: float32 [128, 1024], P('pair', 'virt')
Inputs may be any that keep to these rules, and one draw needn't show every extreme that they name: `kept_groups`: each block names 4 different tile groups; among the blocks of one index of pair each group is named at most 2 times. `owner_table`: a permutation of the tile groups.
All inputs are finite; a program needn't handle non-finite values. No bound on the sum of `tile_mask` on one device may be relied on, other than what follows from the above.
Results may differ from a plain program's by a relative error of at most 0.0003.
Values may be sent and summed in bfloat16 or wider, within the bound.
No kernel may reach another device: no remote copies, remote signals or barrier semaphores. Data moves between devices by JAX's collectives and lax.ppermute only.
A program may use at most 64 MiB of HBM per device.

v0:
```python
import jax
import jax.numpy as jnp
from jax import lax
from jax.sharding import PartitionSpec as P


def local(
    amplitudes,
    kept_groups,
    tile_mask,
    owner_table,
    integrals,
    residual_in,
    pair_energy,
    virt_energy,
):
    block_count = amplitudes.shape[0]
    keep_count = amplitudes.shape[1]
    pair_rows = amplitudes.shape[2]
    group_width = amplitudes.shape[3]
    column_count = integrals.shape[1]
    tile_width = group_width // tile_mask.shape[2]
    group_total = owner_table.shape[0]
    tile_keep = jnp.repeat(tile_mask.astype(amplitudes.dtype), tile_width, axis=2)
    kept_amplitudes = amplitudes * tile_keep[:, :, None, :]
    group_match = kept_groups[:, :, None] == jnp.arange(group_total, dtype=jnp.int32)[None, None, :]
    owner_slots = jnp.sum(jnp.where(group_match, owner_table[None, None, :], 0), axis=2)
    capacity = min(2, block_count)
    task_count = block_count * keep_count
    owners = owner_slots.reshape(task_count)
    targets = jnp.arange(group_total, dtype=jnp.int32)
    to_owner = (owners[:, None] == targets[None, :]).astype(jnp.int32)
    earlier = jnp.cumsum(to_owner, axis=0) - to_owner
    ranking = jnp.sum(earlier * to_owner, axis=1)
    places = jnp.arange(capacity, dtype=jnp.int32)
    placing = (to_owner.T[:, None, :] == 1) & (ranking[None, None, :] == places[None, :, None])
    task_rows = kept_amplitudes.reshape(task_count, pair_rows * group_width)
    outgoing = jnp.einsum(
        "qct,tw->qcw", placing.astype(jnp.bfloat16), task_rows, preferred_element_type=jnp.float32
    )
    outgoing = outgoing.astype(jnp.bfloat16).reshape(group_total, capacity, pair_rows, group_width)
    task_block = jnp.arange(task_count, dtype=jnp.int32) // keep_count
    slot_blocks = jnp.sum(jnp.where(placing, task_block[None, None, :] + 1, 0), axis=2) - 1
    block_ids = jnp.arange(block_count, dtype=jnp.int32)
    full_pairs = pair_rows * lax.axis_size("virt")
    source_rows = block_count * full_pairs
    arrived, arrived_blocks = (
        lax.all_to_all(outgoing, "pair", split_axis=0, concat_axis=0, tiled=True),
        lax.all_to_all(slot_blocks, "pair", split_axis=0, concat_axis=0, tiled=True),
    )
    assembled = lax.all_gather(arrived, "virt", axis=2, tiled=True)
    source_count = lax.axis_size("pair") * source_rows // source_rows
    partial_value = jnp.dot(
        assembled.reshape(-1, group_width), integrals, preferred_element_type=jnp.float32
    )
    partial_value = partial_value.reshape(source_count, capacity, full_pairs, column_count)
    picker = (arrived_blocks[:, :, None] == block_ids[None, None, :]).astype(jnp.float32)
    spread = jnp.einsum("scb,scrn->sbrn", picker, partial_value, precision=lax.Precision.HIGHEST)
    ladder = lax.psum_scatter(
        spread.reshape(lax.axis_size("pair") * source_rows, column_count),
        "pair",
        scatter_dimension=0,
        tiled=True,
    )
    denominator = pair_energy[:, None] - virt_energy[None, :]
    return (residual_in.astype(jnp.float32) + ladder) / denominator


def solution(mesh):
    return jax.shard_map(
        local,
        mesh=mesh,
        in_specs=(
            P("pair", None, "virt", None),
            P("pair", None),
            P("pair", None, None),
            P(),
            P("pair", "virt"),
            P("pair", "virt"),
            P("pair"),
            P("virt"),
        ),
        out_specs=P("pair", "virt"),
        check_vma=False,
    )
```

profile of v0, /device:TPU:0, one launch (start us, length us, event | category | flops | bytes accessed | tf_op | source)
XLA Modules:
  0.0 104.1 jit_solution(14591181512066152208)
XLA Ops:
  6.5 0.0 copy-start
  6.5 0.0 copy-start.3
  6.5 0.9 select_reduce_fusion.1
  7.5 0.1 eq.86
  7.6 0.0 copy-done.3
  7.6 0.1 copy.25
  7.7 0.1 broadcast_in_dim.43
  7.8 0.1 mul.14
  7.9 0.6 copy-done.2
  8.5 0.1 convert_compare_fusion
  8.6 0.2 select_reduce_fusion
  8.8 0.1 fusion
  8.9 0.6 copy.26
  9.5 7.3 %all-to-all-start.1 = ((bf16[8,2,2,128]{3,2,1,0:T(2,128)(2,1)}), bf16[8,2,2,128]{3,2,1,0:T(2,128)(2,1)S(1)}, u32[]{:S(2)}, u32[]{:S(2)}) async-start(bf16[8,2,2,128]{3,2,1,0:T(2,128)(2,1)} %copy.26), calls=%async_computation.1 | async-start | bytes 16384 | tf_op jit(solution)/shard_map/all_to_all | solution.py:48
  16.8 0.1 fusion.8
  16.9 0.7 copy.22
  17.6 5.7 %all-to-all-done.1 = bf16[8,2,2,128]{3,2,1,0:T(2,128)(2,1)S(1)} async-done(((bf16[8,2,2,128]{3,2,1,0:T(2,128)(2,1)}), bf16[8,2,2,128]{3,2,1,0:T(2,128)(2,1)S(1)}, u32[]{:S(2)}, u32[]{:S(2)}) %all-to-all-start.1) | async-done | bytes 8224 | tf_op jit(solution)/shard_map/all_to_all | solution.py:48
  23.3 3.3 %all-to-all-start = ((s32[8,1,2]{2,1,0:T(1,128)}), s32[8,1,2]{2,1,0:T(1,128)S(1)}, u32[]{:S(2)}, u32[]{:S(2)}) async-start(s32[8,1,2]{2,1,0:T(1,128)} %copy.22), calls=%async_computation | async-start | bytes 8192 | tf_op jit(solution)/shard_map/all_to_all | solution.py:49
  26.6 0.0 reduce-scatter.2.cloned.1.call-start
  26.7 5.2 %all_gather.3 = bf16[8,2,8,128]{3,0,2,1:T(8,128)(2,1)S(1)} all-gather(bf16[8,2,2,128]{3,0,2,1:T(8,128)(2,1)S(1)} %copy.27), channel_id=1, replica_groups=mesh['pair'=8,'virt'=4] {'virt'}, dimensions={2}, use_global_device_ids=true | all-gather | bytes 40960 | tf_op jit(solution)/shard_map/all_gather | solution.py:51
  31.9 0.0 copy-done
  31.9 0.2 fusion.3
  32.0 1.0 all-to-all-done
  33.0 0.4 fusion.1
  33.5 0.6 copy.29
  34.1 0.0 copy-start.1
  34.1 0.0 reduce-scatter.2.cloned.1.call-update
  34.1 61.8 %reduce-scatter.2.cloned.1.call-done = f32[16,256]{1,0:T(8,128)} async-done(((f32[128,256]{1,0:T(8,128)}), f32[16,256]{1,0:T(8,128)}) %reduce-scatter.2.cloned.1.call-update) | async-done | bytes 16400 | tf_op jit(solution)/shard_map/reduce_scatter | solution.py:59
  95.9 0.0 copy-done.1
  95.9 0.0 copy-done.4
  95.9 0.0 copy-done.5
  95.9 1.4 %subtract_divide_fusion = f32[16,256]{1,0:T(8,128)} fusion(f32[16,256]{1,0:T(8,128)} %reduce-scatter.2.cloned.1.call-done, bf16[16,256]{1,0:T(8,128)(2,1)S(1)} %copy-done.1, f32[256]{0:T(256)S(1)} %copy-done.4, f32[16]{0:T(128)S(1)} %copy-done.5), kind=kLoop, calls=%fused_computation.6 | loop fusion | flops 16384 | bytes 42048 | tf_op jit(solution)/shard_map/div | solution.py:66
  (11 shorter events, 0.1 us)
Async XLA Ops:
  6.5 25.4 %copy-start = (bf16[128,256]{1,0:T(8,128)(2,1)S(1)}, bf16[128,256]{1,0:T(8,128)(2,1)}, u32[]{:S(2)}) copy-start(bf16[128,256]{1,0:T(8,128)(2,1)} %param.12) | copy-start | bytes 196612
  6.5 1.0 copy-start.3
  7.8 0.7 copy-start.2
  9.5 13.8 %all-to-all-start.1 = ((bf16[8,2,2,128]{3,2,1,0:T(2,128)(2,1)}), bf16[8,2,2,128]{3,2,1,0:T(2,128)(2,1)S(1)}, u32[]{:S(2)}, u32[]{:S(2)}) async-start(bf16[8,2,2,128]{3,2,1,0:T(2,128)(2,1)} %copy.26), calls=%async_computation.1 | async-start | bytes 16384 | tf_op jit(solution)/shard_map/all_to_all | solution.py:48
  23.3 9.7 %all-to-all-start = ((s32[8,1,2]{2,1,0:T(1,128)}), s32[8,1,2]{2,1,0:T(1,128)S(1)}, u32[]{:S(2)}, u32[]{:S(2)}) async-start(s32[8,1,2]{2,1,0:T(1,128)} %copy.22), calls=%async_computation | async-start | bytes 8192 | tf_op jit(solution)/shard_map/all_to_all | solution.py:49
  26.6 69.3 %reduce-scatter.2.cloned.1.call-start = ((), (), s32[]{:S(2)}) async-start(), calls=%async_computation.3 | async-start | bytes 147456 | tf_op jit(solution)/shard_map/reduce_scatter | solution.py:59
  34.1 61.8 %copy-start.1 = (bf16[16,256]{1,0:T(8,128)(2,1)S(1)}, bf16[16,256]{1,0:T(8,128)(2,1)}, u32[]{:S(2)}) copy-start(bf16[16,256]{1,0:T(8,128)(2,1)} %param.13) | copy-start | bytes 24580
  34.1 61.8 %copy-start.4 = (f32[256]{0:T(256)S(1)}, f32[256]{0:T(256)}, u32[]{:S(2)}) copy-start(f32[256]{0:T(256)} %param.15) | copy-start | bytes 3076
  34.1 61.8 %copy-start.5 = (f32[16]{0:T(128)S(1)}, f32[16]{0:T(128)}, u32[]{:S(2)}) copy-start(f32[16]{0:T(128)} %param.14) | copy-start | bytes 196
Sparse Core Ops, SparseCore 0:
  34.3 61.5 reduce-scatter.1
where the time goes:
time: 105 us; the launch traced here: 104 us
  waiting for transfers between devices  68.4 us (65%)
  between operations  13.4 us (13%)
  starting transfers between devices  10.6 us (10%)
  blocking collectives  5.19 us (5%)
  local copies, waits for them, and re-layouts  2.95 us (3%)
  other arithmetic  2.81 us (3%)
    reduce_scatter x1, waiting for transfers between devices, local(): lax.psum_scatter(spread.reshape(lax.axis_size('pair') * source_rows, colu...  61.8 us
    all_to_all x1, starting transfers between devices, local(): lax.all_to_all(outgoing, 'pair', split_axis=0, concat_axis=0, tiled=True)  7.25 us
    all_to_all x1, waiting for transfers between devices, local(): lax.all_to_all(outgoing, 'pair', split_axis=0, concat_axis=0, tiled=True)  5.67 us
    all_gather x1, blocking collectives, local(): assembled = lax.all_gather(arrived, 'virt', axis=2, tiled=True)  5.19 us
    all_to_all x1, starting transfers between devices, local(): lax.all_to_all(slot_blocks, 'pair', split_axis=0, concat_axis=0, tiled=True)  3.33 us
  transfers between devices with their start and end apart: 3, of which 3 were waited for; matrix products, arithmetic and copies ran while one was open for 1% of the time, Pallas kernels for 0%

commit v1 on v0

v1 whole, which is shorter than its diff:
```python
import functools
import math

import jax
import jax.numpy as jnp
from jax import lax
from jax.experimental import pallas as pl
from jax.experimental.pallas import tpu as pltpu
from jax.sharding import PartitionSpec as P

OUTER_BIT = 0


def relative_place(slot, me, bits):
    apart = slot ^ me
    place = jnp.int32(0)
    for at, bit in enumerate(bits):
        place = place | (((apart >> bit) & 1) << at)
    return place


def spread_kernel(bits, kept_ref, mask_ref, owner_ref, amp_ref, out_ref, rows_ref):
    blocks, keep, pair_rows, width = amp_ref.shape
    tiles = mask_ref.shape[1]
    me = lax.axis_index("pair")
    lane_tile = lax.broadcasted_iota(jnp.int32, (pair_rows, width), 1) // (width // tiles)
    out_rows = out_ref.shape[0]
    tasks = blocks * keep
    row = lax.broadcasted_iota(jnp.int32, (out_rows, tasks * pair_rows), 0)
    column = lax.broadcasted_iota(jnp.int32, (out_rows, tasks * pair_rows), 1)
    wanted = jnp.full((out_rows, tasks * pair_rows), -1, jnp.int32)
    for b in range(blocks):
        for k in range(keep):
            task = b * keep + k
            place = relative_place(owner_ref[kept_ref[b, k]], me, bits)
            first = (place * blocks + b) * pair_rows
            wanted = jnp.where(column // pair_rows == task, first + column % pair_rows, wanted)
            scale = jnp.zeros((pair_rows, width), jnp.float32)
            for s in range(tiles):
                scale = jnp.where(lane_tile == s, mask_ref[b, s, k].astype(jnp.float32), scale)
            rows_ref[pl.ds(task * pair_rows, pair_rows), :] = amp_ref[b, k].astype(jnp.float32) * scale
    pick = (row == wanted).astype(jnp.bfloat16)
    out_ref[...] = jnp.dot(
        pick, rows_ref[...].astype(jnp.bfloat16), preferred_element_type=jnp.float32
    ).astype(out_ref.dtype)


def spread(amplitudes, kept_groups, tile_mask, owner_table, bits):
    blocks, keep, pair_rows, width = amplitudes.shape
    out_rows = owner_table.shape[0] * blocks * pair_rows
    smem = pl.BlockSpec(memory_space=pltpu.SMEM)
    vmem = pl.BlockSpec(memory_space=pltpu.VMEM)
    return pl.pallas_call(
        functools.partial(spread_kernel, bits),
        out_shape=jax.ShapeDtypeStruct((out_rows, width), amplitudes.dtype),
        in_specs=[smem, smem, smem, vmem],
        out_specs=vmem,
        scratch_shapes=[pltpu.VMEM((blocks * keep * pair_rows, width), jnp.float32)],
        name="spread",
    )(kept_groups, jnp.swapaxes(tile_mask, 1, 2), owner_table, amplitudes)


def share_of(blocks, pair_rows, lhs, blocks_of_integrals):
    virt_size = lhs.shape[0] // (len(blocks_of_integrals) * blocks * pair_rows)
    full_rows = virt_size * pair_rows
    inner = len(blocks_of_integrals)
    me = lax.axis_index("virt")
    row = lax.broadcasted_iota(jnp.int32, (blocks * full_rows, lhs.shape[0]), 0)
    column = lax.broadcasted_iota(jnp.int32, (blocks * full_rows, lhs.shape[0]), 1)
    block, pair = row // full_rows, row % full_rows
    piece = (pair // pair_rows) ^ me
    total = None
    for t in range(inner):
        wanted = ((piece * inner + t) * blocks + block) * pair_rows + pair % pair_rows
        pick = (column == wanted).astype(jnp.bfloat16)
        left = jnp.dot(pick, lhs, preferred_element_type=jnp.float32).astype(jnp.bfloat16)
        term = jnp.dot(left, blocks_of_integrals[t], preferred_element_type=jnp.float32)
        total = term if total is None else total + term
    return total


def far_kernel(blocks, pair_rows, lhs_ref, *refs):
    *integral_refs, out_ref = refs
    held = [r[t] for r in integral_refs for t in range(r.shape[0])]
    out_ref[...] = share_of(blocks, pair_rows, lhs_ref[...], held)


def near_kernel(blocks, pair_rows, lhs_ref, residual_ref, pair_ref, virt_ref, *refs):
    *integral_refs, top_ref, under_ref = refs
    held = [r[t] for r in integral_refs for t in range(r.shape[0])]
    total = share_of(blocks, pair_rows, lhs_ref[...], held)
    top_ref[...] = residual_ref[...].astype(jnp.float32) + total
    rows = total.shape[0]
    here = lax.broadcasted_iota(jnp.int32, (rows, rows), 0)
    there = lax.broadcasted_iota(jnp.int32, (rows, rows), 1)
    pair_column = jnp.sum(jnp.where(here == there, pair_ref[...], 0.0), axis=1, keepdims=True)
    under_ref[...] = pair_column - virt_ref[...]


def swap(x, axis_name, bit):
    size = lax.axis_size(axis_name)
    return lax.ppermute(x, axis_name, [(i, i ^ (1 << bit)) for i in range(size)])


def local(
    amplitudes,
    kept_groups,
    tile_mask,
    owner_table,
    integrals,
    residual_in,
    pair_energy,
    virt_energy,
):
    blocks, _, pair_rows, width = amplitudes.shape
    columns = integrals.shape[1]
    pair_bits = (lax.axis_size("pair") - 1).bit_length()
    virt_bits = (lax.axis_size("virt") - 1).bit_length()
    inner_bits = [b for b in reversed(range(pair_bits)) if b != OUTER_BIT]
    bits = tuple(inner_bits) + (OUTER_BIT,)
    vmem = pl.BlockSpec(memory_space=pltpu.VMEM)

    held = integrals[None]
    spread_rows = spread(amplitudes, kept_groups, tile_mask, owner_table, bits)
    half = spread_rows.shape[0] // 2
    pieces = spread_rows.reshape(2, half, width)
    for bit in inner_bits:
        held = jnp.concatenate([held, swap(held, "pair", bit)], axis=0)
    for bit in range(virt_bits):
        pieces = jnp.concatenate([pieces, swap(pieces, "virt", bit)], axis=1)
    far_rows = swap(pieces[1], "pair", OUTER_BIT)
    rows = residual_in.shape[0]
    far = pl.pallas_call(
        functools.partial(far_kernel, blocks, pair_rows),
        out_shape=jax.ShapeDtypeStruct((rows, columns), jnp.float32),
        in_specs=[vmem] * 2,
        out_specs=vmem,
        name="far",
    )(far_rows, held)
    top, under = pl.pallas_call(
        functools.partial(near_kernel, blocks, pair_rows),
        out_shape=[jax.ShapeDtypeStruct((rows, columns), jnp.float32)] * 2,
        in_specs=[vmem] * 5,
        out_specs=[vmem] * 2,
        name="near",
    )(pieces[0], residual_in, pair_energy[None, :], virt_energy[None, :], held)
    return (top + swap(far, "pair", OUTER_BIT)) / under


def general(
    amplitudes,
    kept_groups,
    tile_mask,
    owner_table,
    integrals,
    residual_in,
    pair_energy,
    virt_energy,
):
    block_count = amplitudes.shape[0]
    keep_count = amplitudes.shape[1]
    pair_rows = amplitudes.shape[2]
    group_width = amplitudes.shape[3]
    column_count = integrals.shape[1]
    tile_width = group_width // tile_mask.shape[2]
    group_total = owner_table.shape[0]
    tile_keep = jnp.repeat(tile_mask.astype(amplitudes.dtype), tile_width, axis=2)
    kept_amplitudes = amplitudes * tile_keep[:, :, None, :]
    group_match = kept_groups[:, :, None] == jnp.arange(group_total, dtype=jnp.int32)[None, None, :]
    owner_slots = jnp.sum(jnp.where(group_match, owner_table[None, None, :], 0), axis=2)
    placing = owner_slots[:, None, :] == jnp.arange(group_total, dtype=jnp.int32)[None, :, None]
    outgoing = jnp.einsum(
        "bqk,bkrw->qbrw", placing.astype(jnp.bfloat16), kept_amplitudes, preferred_element_type=jnp.float32
    ).astype(jnp.bfloat16)
    full_pairs = pair_rows * lax.axis_size("virt")
    arrived = lax.all_to_all(outgoing, "pair", split_axis=0, concat_axis=0, tiled=True)
    assembled = lax.all_gather(arrived, "virt", axis=2, tiled=True)
    partial_value = jnp.dot(
        assembled.reshape(-1, group_width), integrals, preferred_element_type=jnp.float32
    )
    ladder = lax.psum_scatter(partial_value, "pair", scatter_dimension=0, tiled=True)
    denominator = pair_energy[:, None] - virt_energy[None, :]
    return (residual_in.astype(jnp.float32) + ladder) / denominator


def solution(mesh):
    sizes = dict(mesh.shape)
    regular = all(s & (s - 1) == 0 for s in sizes.values()) and sizes["pair"] <= 8
    return jax.shard_map(
        local if regular else general,
        mesh=mesh,
        in_specs=(
            P("pair", None, "virt", None),
            P("pair", None),
            P("pair", None, None),
            P(),
            P("pair", "virt"),
            P("pair", "virt"),
            P("pair"),
            P("virt"),
        ),
        out_specs=P("pair", "virt"),
        check_vma=False,
    )
```

time: 105 us -> 27.6 us (0.26)
  waiting for transfers between devices: 68.4 us -> 7.31 us
  between operations: 13.4 us -> 0.02 us
  Pallas kernels: 0 us -> 5.59 us
  blocking collectives: 5.19 us -> 0 us
  local copies, waits for them, and re-layouts: 2.95 us -> 1.21 us
  starting transfers between devices: 10.6 us -> 9.41 us
    reduce_scatter x1 -> x0, waiting for transfers between devices: 61.8 us -> none  [local(): lax.psum_scatter(spread.reshape(lax.axis_size('pair') * source_rows, colu...]
    all_to_all x2 -> x0, starting transfers between devices: 10.6 us -> none  [the longest x1 7.25 us: local(): lax.all_to_all(outgoing, 'pair', split_axis=0, concat_axis=0, tiled=True)]
    ppermute x0 -> x6, starting transfers between devices: none -> 9.41 us  [swap(): return lax.ppermute(x, axis_name, [(i, i ^ 1 << bit) for i in range(size)])]
    ppermute x0 -> x6, waiting for transfers between devices: none -> 7.31 us  [swap(): return lax.ppermute(x, axis_name, [(i, i ^ 1 << bit) for i in range(size)])]
    all_to_all x2 -> x0, waiting for transfers between devices: 6.67 us -> none  [the longest x1 5.67 us: local(): lax.all_to_all(outgoing, 'pair', split_axis=0, concat_axis=0, tiled=True)]
    pallas_call x0 -> x3, Pallas kernels: none -> 5.59 us  [the longest x1 2.01 us: local(): pl.pallas_call(functools.partial(near_kernel, blocks, pair_rows), out_sha...]
    all_gather x1 -> x0, blocking collectives: 5.19 us -> none  [local(): assembled = lax.all_gather(arrived, 'virt', axis=2, tiled=True)]
    concatenate x0 -> x4, other arithmetic: none -> 2.14 us  [the longest x2 1.4 us: local(): pieces = jnp.concatenate([pieces, swap(pieces, 'virt', bit)], axis=1)]
  transfers between devices with their start and end apart: 3 -> 6, of which waited for: 3 -> 4; matrix products, arithmetic and copies ran while one was open for 1% -> 8% of each run, Pallas kernels for 0% -> 7%
where the time goes in v1:
time: 27.6 us; the launch traced here: 27 us
  starting transfers between devices  9.41 us (34%)
  waiting for transfers between devices  7.31 us (26%)
  Pallas kernels  5.59 us (20%)
  other arithmetic  3.49 us (13%)
  local copies, waits for them, and re-layouts  1.21 us (4%)
    ppermute x6, starting transfers between devices, swap(): return lax.ppermute(x, axis_name, [(i, i ^ 1 << bit) for i in range(size)])  9.41 us
    ppermute x6, waiting for transfers between devices, swap(): return lax.ppermute(x, axis_name, [(i, i ^ 1 << bit) for i in range(size)])  7.31 us
    pallas_call x1, Pallas kernels, local(): pl.pallas_call(functools.partial(near_kernel, blocks, pair_rows), out_sha...  2.01 us
    pallas_call x1, Pallas kernels, local(): pl.pallas_call(functools.partial(far_kernel, blocks, pair_rows), out_shap...  1.96 us
    pallas_call x1, Pallas kernels, spread(): pl.pallas_call(functools.partial(spread_kernel, bits), out_shape=jax.Shap...  1.62 us
    concatenate x2, other arithmetic, local(): pieces = jnp.concatenate([pieces, swap(pieces, 'virt', bit)], axis=1)  1.4 us
    div x1, other arithmetic, local(): return (top + swap(far, 'pair', OUTER_BIT)) / under  1.35 us
    concatenate x2, other arithmetic, local(): held = jnp.concatenate([held, swap(held, 'pair', bit)], axis=0)  0.74 us
  transfers between devices with their start and end apart: 6, of which 4 were waited for; matrix products, arithmetic and copies ran while one was open for 8% of the time, Pallas kernels for 7%

profile of v1, /device:TPU:0, one launch (start us, length us, event | category | flops | bytes accessed | tf_op | source)
XLA Modules:
  0.0 27.0 jit_solution(14090585218725873118)
XLA Ops:
  0.0 0.0 copy-start
  0.0 1.6 %spread.1 = bf16[32,128]{1,0:T(8,128)(2,1)} custom-call(s32[2,4]{1,0:T(2,128)} %kept_ref.1, s32[2,2,4]{2,1,0:T(2,128)} %bitcast.15, s32[8]{0:T(128)} %owner_ref.1, bf16[2,4,2,128]{3,2,1,0:T(2,128)(2,1)} %amp_ref.1), custom_call_target="tpu_custom_call" | custom-call | tf_op jit(solution)/shard_map/spread/pallas_call | solution.py:53
  1.6 0.5 %collective-permute-start = (bf16[2,16,128]{2,1,0:T(8,128)(2,1)}, bf16[2,16,128]{2,1,0:T(8,128)(2,1)S(1)}, u32[]{:S(2)}, u32[]{:S(2)}) collective-permute-start(bf16[2,16,128]{2,1,0:T(8,128)(2,1)} %bitcast.12), channel_id=1, source_target_pairs={{0,1},{1,0},{2,3},{3,2},{4,5},{5,4},{6,7},{7,6},{8,9},{9,8},{10,11... | collective-permute-start | bytes 24584 | tf_op jit(solution)/shard_map/ppermute | solution.py:102
  2.1 1.0 %collective-permute-done = bf16[2,16,128]{2,1,0:T(8,128)(2,1)S(1)} collective-permute-done((bf16[2,16,128]{2,1,0:T(8,128)(2,1)}, bf16[2,16,128]{2,1,0:T(8,128)(2,1)S(1)}, u32[]{:S(2)}, u32[]{:S(2)}) %collective-permute-start) | collective-permute-done | bytes 8224 | tf_op jit(solution)/shard_map/ppermute | solution.py:102
  3.1 0.7 %pad_maximum_fusion.3 = bf16[2,32,128]{2,1,0:T(8,128)(2,1)S(1)} fusion(bf16[2,16,128]{2,1,0:T(8,128)(2,1)S(1)} %collective-permute-done, bf16[2,16,128]{2,1,0:T(8,128)(2,1)} %bitcast.13), kind=kLoop, calls=%fused_computation.5 | loop fusion | flops 32768 | bytes 32768 | tf_op jit(solution)/shard_map/concatenate | solution.py:130
  3.8 2.9 %collective-permute-start.1 = (bf16[2,32,128]{2,1,0:T(8,128)(2,1)S(1)}, bf16[2,32,128]{2,1,0:T(8,128)(2,1)S(1)}, u32[]{:S(2)}, u32[]{:S(2)}) collective-permute-start(bf16[2,32,128]{2,1,0:T(8,128)(2,1)S(1)} %pad_maximum_fusion.3), channel_id=1, source_target_pairs={{0,2},{1,3},{2,0},{3,1},{4,6},{5,7},{6,4},{7,5},{8,10},{9,11},{10,... | collective-permute-start | bytes 49160 | tf_op jit(solution)/shard_map/ppermute | solution.py:102
  6.7 2.6 %collective-permute-start.2 = (bf16[1,128,256]{2,1,0:T(8,128)(2,1)}, bf16[1,128,256]{2,1,0:T(8,128)(2,1)S(1)}, u32[]{:S(2)}, u32[]{:S(2)}) collective-permute-start(bf16[1,128,256]{2,1,0:T(8,128)(2,1)} %bitcast.9), channel_id=1, source_target_pairs={{0,16},{4,20},{8,24},{12,28},{16,0},{20,4},{24,8},{28,12},{1,17},{... | collective-permute-start | bytes 196616 | tf_op jit(solution)/shard_map/ppermute | solution.py:102
  9.3 0.0 collective-permute-done.1
  9.3 0.7 %pad_maximum_fusion.2 = bf16[2,64,128]{2,1,0:T(8,128)(2,1)S(1)} fusion(bf16[2,32,128]{2,1,0:T(8,128)(2,1)S(1)} %collective-permute-done.1, bf16[2,16,128]{2,1,0:T(8,128)(2,1)S(1)} %collective-permute-done, bf16[2,16,128]{2,1,0:T(8,128)(2,1)} %bitcast.14), kind=kLoop, calls=%fused_computation.2 | loop fusion | flops 98304 | bytes 65536 | tf_op jit(solution)/shard_map/concatenate | solution.py:130
  10.0 3.4 %collective-permute-done.2 = bf16[1,128,256]{2,1,0:T(8,128)(2,1)S(1)} collective-permute-done((bf16[1,128,256]{2,1,0:T(8,128)(2,1)}, bf16[1,128,256]{2,1,0:T(8,128)(2,1)S(1)}, u32[]{:S(2)}, u32[]{:S(2)}) %collective-permute-start.2) | collective-permute-done | bytes 65568 | tf_op jit(solution)/shard_map/ppermute | solution.py:102
  13.4 0.0 copy-done
  13.4 0.5 %collective-permute-start.3 = (bf16[2,128,256]{2,1,0:T(8,128)(2,1)S(1)}, bf16[2,128,256]{2,1,0:T(8,128)(2,1)S(1)}, u32[]{:S(2)}, u32[]{:S(2)}) collective-permute-start(bf16[2,128,256]{2,1,0:T(8,128)(2,1)S(1)} %pad_maximum_fusion.1), channel_id=1, source_target_pairs={{0,8},{4,12},{8,0},{12,4},{16,24},{20,28},{24,16},{28,20},{1,9},{5... | collective-permute-start | bytes 393224 | tf_op jit(solution)/shard_map/ppermute | solution.py:102
  13.9 0.6 %slice_bitcast_fusion = (bf16[64,128]{1,0:T(8,128)(2,1)S(1)}, bf16[64,128]{1,0:T(8,128)(2,1)}) fusion(bf16[2,64,128]{2,1,0:T(8,128)(2,1)S(1)} %pad_maximum_fusion.2), kind=kLoop, calls=%fused_computation.3 | loop fusion | bytes 65536 | tf_op jit(solution)/shard_map/squeeze | solution.py:131
  14.5 1.5 %collective-permute-start.4 = (bf16[64,128]{1,0:T(8,128)(2,1)S(1)}, bf16[64,128]{1,0:T(8,128)(2,1)S(1)}, u32[]{:S(2)}, u32[]{:S(2)}) collective-permute-start(bf16[64,128]{1,0:T(8,128)(2,1)S(1)} %get-tuple-element.9), channel_id=1, source_target_pairs={{0,4},{4,0},{8,12},{12,8},{16,20},{20,16},{24,28},{28,24},{1,5},{5... | collective-permute-start | bytes 49160 | tf_op jit(solution)/shard_map/ppermute | solution.py:102
  16.0 2.4 %collective-permute-done.3 = bf16[2,128,256]{2,1,0:T(8,128)(2,1)S(1)} collective-permute-done((bf16[2,128,256]{2,1,0:T(8,128)(2,1)S(1)}, bf16[2,128,256]{2,1,0:T(8,128)(2,1)S(1)}, u32[]{:S(2)}, u32[]{:S(2)}) %collective-permute-start.3) | collective-permute-done | bytes 131104 | tf_op jit(solution)/shard_map/ppermute | solution.py:102
  18.4 0.7 %pad_maximum_fusion.refs_0_ = bf16[4,128,256]{2,1,0:T(8,128)(2,1)} fusion(bf16[2,128,256]{2,1,0:T(8,128)(2,1)S(1)} %collective-permute-done.3, bf16[1,128,256]{2,1,0:T(8,128)(2,1)S(1)} %collective-permute-done.2, bf16[1,128,256]{2,1,0:T(8,128)(2,1)S(1)} %bitcast.11), kind=kLoop, calls=%fused_computation | loop fusion | flops 262144 | bytes 524288 | tf_op jit(solution)/shard_map/concatenate | solution.py:128
  19.2 0.0 collective-permute-done.4.lhs_ref
  19.2 0.0 copy-start.1
  19.2 0.6 %copy-done.1 = bf16[64,128]{1,0:T(8,128)(2,1)} copy-done((bf16[64,128]{1,0:T(8,128)(2,1)}, bf16[64,128]{1,0:T(8,128)(2,1)S(1)}, u32[]{:S(2)}) %copy-start.1) | copy-done | bytes 16408
  19.8 2.0 %far.1 = f32[16,256]{1,0:T(8,128)} custom-call(bf16[64,128]{1,0:T(8,128)(2,1)} %copy-done.1, bf16[4,128,256]{2,1,0:T(8,128)(2,1)} %pad_maximum_fusion.refs_0_), custom_call_target="tpu_custom_call" | custom-call | tf_op jit(solution)/shard_map/far/pallas_call | solution.py:133
  21.7 1.5 %collective-permute-start.5 = (f32[16,256]{1,0:T(8,128)}, f32[16,256]{1,0:T(8,128)S(1)}, u32[]{:S(2)}, u32[]{:S(2)}) collective-permute-start(f32[16,256]{1,0:T(8,128)} %far.1), channel_id=1, source_target_pairs={{0,4},{4,0},{8,12},{12,8},{16,20},{20,16},{24,28},{28,24},{1,5},{5... | collective-permute-start | bytes 49160 | tf_op jit(solution)/shard_map/ppermute | solution.py:102
  23.2 2.0 %near.1 = (f32[16,256]{1,0:T(8,128)}, f32[16,256]{1,0:T(8,128)}) custom-call(bf16[64,128]{1,0:T(8,128)(2,1)} %get-tuple-element.10.lhs_ref, bf16[16,256]{1,0:T(8,128)(2,1)} %residual_ref.1, f32[1,16]{1,0:T(1,128)} %bitcast.17, f32[1,256]{1,0:T(1,128)} %bitcast.16, bf16[4,128,256]{2,1,0:T(8,128)(2,1)} %pad_maximum_fusion.refs_0_), custom_call_target="tpu_custom_call" | custom-call | tf_op jit(solution)/shard_map/near/pallas_call | solution.py:140
  25.2 0.4 %collective-permute-done.5 = f32[16,256]{1,0:T(8,128)S(1)} collective-permute-done((f32[16,256]{1,0:T(8,128)}, f32[16,256]{1,0:T(8,128)S(1)}, u32[]{:S(2)}, u32[]{:S(2)}) %collective-permute-start.5) | collective-permute-done | bytes 16416 | tf_op jit(solution)/shard_map/ppermute | solution.py:102
  25.7 1.3 %add_divide_fusion = f32[16,256]{1,0:T(8,128)} fusion(f32[16,256]{1,0:T(8,128)} %get-tuple-element.8, f32[16,256]{1,0:T(8,128)} %get-tuple-element.7, f32[16,256]{1,0:T(8,128)S(1)} %collective-permute-done.5), kind=kLoop, calls=%fused_computation.6 | loop fusion | flops 8192 | bytes 65536 | tf_op jit(solution)/shard_map/div | solution.py:147
  (1 shorter events, 0.0 us)
Async XLA Ops:
  0.0 13.4 %copy-start = (bf16[128,256]{1,0:T(8,128)(2,1)S(1)}, bf16[128,256]{1,0:T(8,128)(2,1)}, u32[]{:S(2)}) copy-start(bf16[128,256]{1,0:T(8,128)(2,1)} %param.12) | copy-start | bytes 196612
  1.6 1.5 %collective-permute-start = (bf16[2,16,128]{2,1,0:T(8,128)(2,1)}, bf16[2,16,128]{2,1,0:T(8,128)(2,1)S(1)}, u32[]{:S(2)}, u32[]{:S(2)}) collective-permute-start(bf16[2,16,128]{2,1,0:T(8,128)(2,1)} %bitcast.12), channel_id=1, source_target_pairs={{0,1},{1,0},{2,3},{3,2},{4,5},{5,4},{6,7},{7,6},{8,9},{9,8},{10,11... | collective-permute-start | bytes 24584 | tf_op jit(solution)/shard_map/ppermute | solution.py:102
  3.8 5.5 %collective-permute-start.1 = (bf16[2,32,128]{2,1,0:T(8,128)(2,1)S(1)}, bf16[2,32,128]{2,1,0:T(8,128)(2,1)S(1)}, u32[]{:S(2)}, u32[]{:S(2)}) collective-permute-start(bf16[2,32,128]{2,1,0:T(8,128)(2,1)S(1)} %pad_maximum_fusion.3), channel_id=1, source_target_pairs={{0,2},{1,3},{2,0},{3,1},{4,6},{5,7},{6,4},{7,5},{8,10},{9,11},{10,... | collective-permute-start | bytes 49160 | tf_op jit(solution)/shard_map/ppermute | solution.py:102
  6.7 6.7 %collective-permute-start.2 = (bf16[1,128,256]{2,1,0:T(8,128)(2,1)}, bf16[1,128,256]{2,1,0:T(8,128)(2,1)S(1)}, u32[]{:S(2)}, u32[]{:S(2)}) collective-permute-start(bf16[1,128,256]{2,1,0:T(8,128)(2,1)} %bitcast.9), channel_id=1, source_target_pairs={{0,16},{4,20},{8,24},{12,28},{16,0},{20,4},{24,8},{28,12},{1,17},{... | collective-permute-start | bytes 196616 | tf_op jit(solution)/shard_map/ppermute | solution.py:102
  13.4 5.0 %collective-permute-start.3 = (bf16[2,128,256]{2,1,0:T(8,128)(2,1)S(1)}, bf16[2,128,256]{2,1,0:T(8,128)(2,1)S(1)}, u32[]{:S(2)}, u32[]{:S(2)}) collective-permute-start(bf16[2,128,256]{2,1,0:T(8,128)(2,1)S(1)} %pad_maximum_fusion.1), channel_id=1, source_target_pairs={{0,8},{4,12},{8,0},{12,4},{16,24},{20,28},{24,16},{28,20},{1,9},{5... | collective-permute-start | bytes 393224 | tf_op jit(solution)/shard_map/ppermute | solution.py:102
  14.5 4.6 %collective-permute-start.4 = (bf16[64,128]{1,0:T(8,128)(2,1)S(1)}, bf16[64,128]{1,0:T(8,128)(2,1)S(1)}, u32[]{:S(2)}, u32[]{:S(2)}) collective-permute-start(bf16[64,128]{1,0:T(8,128)(2,1)S(1)} %get-tuple-element.9), channel_id=1, source_target_pairs={{0,4},{4,0},{8,12},{12,8},{16,20},{20,16},{24,28},{28,24},{1,5},{5... | collective-permute-start | bytes 49160 | tf_op jit(solution)/shard_map/ppermute | solution.py:102
  19.2 0.6 %copy-start.1 = (bf16[64,128]{1,0:T(8,128)(2,1)}, bf16[64,128]{1,0:T(8,128)(2,1)S(1)}, u32[]{:S(2)}) copy-start(bf16[64,128]{1,0:T(8,128)(2,1)S(1)} %collective-permute-done.4.lhs_ref) | copy-start | bytes 49156
  21.7 3.9 %collective-permute-start.5 = (f32[16,256]{1,0:T(8,128)}, f32[16,256]{1,0:T(8,128)S(1)}, u32[]{:S(2)}, u32[]{:S(2)}) collective-permute-start(f32[16,256]{1,0:T(8,128)} %far.1), channel_id=1, source_target_pairs={{0,4},{4,0},{8,12},{12,8},{16,20},{20,16},{24,28},{28,24},{1,5},{5... | collective-permute-start | bytes 49160 | tf_op jit(solution)/shard_map/ppermute | solution.py:102

commit v2 on v1

v2 whole, which is shorter than its diff:
```python
import functools
import math

import jax
import jax.numpy as jnp
from jax import lax
from jax.experimental import pallas as pl
from jax.experimental.pallas import tpu as pltpu
from jax.sharding import PartitionSpec as P

KERNEL_VMEM = 1 << 20
STEPS = [(4, [0]), (1, [0, 4]), (2, [0, 4]), (3, [0, 4])]


def prepare_kernel(
    kept_hbm,
    mask_hbm,
    owner_hbm,
    amp_hbm,
    integrals_hbm,
    residual_hbm,
    pair_hbm,
    virt_hbm,
    rows_ref,
    own_ref,
    residual_ref,
    under_ref,
    kept_ref,
    mask_ref,
    owner_ref,
    amp_ref,
    rest_ref,
    pair_ref,
    virt_ref,
    kept_rows_ref,
    sems,
):
    moves = [
        pltpu.make_async_copy(source, target, sems.at[n])
        for n, (source, target) in enumerate(
            (
                (kept_hbm, kept_ref),
                (mask_hbm, mask_ref),
                (owner_hbm, owner_ref),
                (amp_hbm, amp_ref),
                (integrals_hbm, own_ref.at[0]),
                (residual_hbm, rest_ref),
                (pair_hbm, pair_ref),
                (virt_hbm, virt_ref),
            )
        )
    ]
    for move in moves:
        move.start()
    blocks, keep, pair_rows, width = amp_ref.shape
    tiles = mask_ref.shape[1]
    me = lax.axis_index("pair")
    lane_tile = lax.broadcasted_iota(jnp.int32, (pair_rows, width), 1) // (width // tiles)
    out_rows = rows_ref.shape[0]
    tasks = blocks * keep
    row = lax.broadcasted_iota(jnp.int32, (out_rows, tasks * pair_rows), 0)
    column = lax.broadcasted_iota(jnp.int32, (out_rows, tasks * pair_rows), 1)
    wanted = jnp.full((out_rows, tasks * pair_rows), -1, jnp.int32)
    for move in moves:
        move.wait()
    for b in range(blocks):
        for k in range(keep):
            task = b * keep + k
            first = ((owner_ref[kept_ref[b, k]] ^ me) * blocks + b) * pair_rows
            wanted = jnp.where(column // pair_rows == task, first + column % pair_rows, wanted)
            scale = jnp.zeros((pair_rows, width), jnp.float32)
            for s in range(tiles):
                scale = jnp.where(lane_tile == s, mask_ref[b, s, k].astype(jnp.float32), scale)
            kept_rows_ref[pl.ds(task * pair_rows, pair_rows), :] = amp_ref[b, k].astype(jnp.float32) * scale
    pick = (row == wanted).astype(jnp.bfloat16)
    rows_ref[...] = jnp.dot(
        pick, kept_rows_ref[...].astype(jnp.bfloat16), preferred_element_type=jnp.float32
    ).astype(rows_ref.dtype)
    residual_ref[...] = rest_ref[...].astype(jnp.float32)
    count = under_ref.shape[0]
    here = lax.broadcasted_iota(jnp.int32, (count, count), 0)
    there = lax.broadcasted_iota(jnp.int32, (count, count), 1)
    pair_column = jnp.sum(jnp.where(here == there, pair_ref[...], 0.0), axis=1, keepdims=True)
    under_ref[...] = pair_column - virt_ref[...]


def prepare(amplitudes, kept_groups, tile_mask, owner_table, integrals, residual_in, pair_energy, virt_energy):
    blocks, keep, pair_rows, width = amplitudes.shape
    out_rows = owner_table.shape[0] * blocks * pair_rows
    operands = (
        kept_groups,
        jnp.swapaxes(tile_mask, 1, 2),
        owner_table,
        amplitudes,
        integrals,
        residual_in,
        pair_energy[None, :],
        virt_energy[None, :],
    )
    operands = [pltpu.with_memory_space_constraint(x, pltpu.HBM) for x in operands]
    scratch = [pltpu.SMEM(x.shape, x.dtype) for x in operands[:3]]
    scratch += [pltpu.VMEM(x.shape, x.dtype) for x in (operands[3], *operands[5:])]
    return pl.pallas_call(
        prepare_kernel,
        out_shape=[
            jax.ShapeDtypeStruct((out_rows, width), amplitudes.dtype),
            jax.ShapeDtypeStruct((1, *integrals.shape), integrals.dtype),
            jax.ShapeDtypeStruct(residual_in.shape, jnp.float32),
            jax.ShapeDtypeStruct(residual_in.shape, jnp.float32),
        ],
        in_specs=[pl.BlockSpec(memory_space=pl.ANY)] * len(operands),
        out_specs=[pl.BlockSpec(memory_space=pltpu.VMEM)] * 4,
        scratch_shapes=scratch
        + [pltpu.VMEM((blocks * keep * pair_rows, width), jnp.float32), pltpu.SemaphoreType.DMA((len(operands),))],
        compiler_params=pltpu.CompilerParams(vmem_limit_bytes=KERNEL_VMEM),
        name="prepare",
    )(*operands)


def share_of(blocks, pair_rows, lhs, blocks_of_integrals):
    virt_size = lhs.shape[0] // (len(blocks_of_integrals) * blocks * pair_rows)
    full_rows = virt_size * pair_rows
    count = len(blocks_of_integrals)
    me = lax.axis_index("virt")
    row = lax.broadcasted_iota(jnp.int32, (blocks * full_rows, lhs.shape[0]), 0)
    column = lax.broadcasted_iota(jnp.int32, (blocks * full_rows, lhs.shape[0]), 1)
    block, pair = row // full_rows, row % full_rows
    piece = (pair // pair_rows) ^ me
    total = None
    for t in range(count):
        wanted = ((piece * count + t) * blocks + block) * pair_rows + pair % pair_rows
        pick = (column == wanted).astype(jnp.bfloat16)
        left = jnp.dot(pick, lhs, preferred_element_type=jnp.float32).astype(jnp.bfloat16)
        term = jnp.dot(left, blocks_of_integrals[t], preferred_element_type=jnp.float32)
        total = term if total is None else total + term
    return total


def update_kernel(blocks, pair_rows, places, lhs_ref, residual_ref, under_ref, *refs):
    *integral_refs, out_ref = refs
    held = [None] * sum(len(p) for p in places)
    for ref, at in zip(integral_refs, places):
        for t, place in enumerate(at):
            held[place] = ref[t]
    total = share_of(blocks, pair_rows, lhs_ref[...], held)
    out_ref[...] = (residual_ref[...] + total) / under_ref[...]


def swap(x, axis_name, mask):
    size = lax.axis_size(axis_name)
    return lax.ppermute(x, axis_name, [(i, i ^ mask) for i in range(size)])


def local(
    amplitudes,
    kept_groups,
    tile_mask,
    owner_table,
    integrals,
    residual_in,
    pair_energy,
    virt_energy,
):
    blocks, _, pair_rows, _ = amplitudes.shape
    vmem = pl.BlockSpec(memory_space=pltpu.VMEM)
    virt_bits = (lax.axis_size("virt") - 1).bit_length()
    rows, own, residual, under = prepare(
        amplitudes, kept_groups, tile_mask, owner_table, integrals, residual_in, pair_energy, virt_energy
    )
    have = {0: own}
    arrays = [(own, (0,))]
    for mask, labels in STEPS:
        sent = [have[l] if (l or len(labels) > 1) else integrals[None] for l in labels]
        sent = sent[0] if len(sent) == 1 else jnp.concatenate(sent, axis=0)
        got = swap(sent, "pair", mask)
        arrays.append((got, tuple(l ^ mask for l in labels)))
        for n, l in enumerate(labels):
            have[l ^ mask] = got if len(labels) == 1 else got[n : n + 1]
    pieces = rows
    for bit in range(virt_bits):
        pieces = jnp.concatenate([pieces, swap(pieces, "virt", 1 << bit)], axis=0)
    return pl.pallas_call(
        functools.partial(update_kernel, blocks, pair_rows, [at for _, at in arrays]),
        out_shape=jax.ShapeDtypeStruct(residual_in.shape, jnp.float32),
        in_specs=[vmem] * (3 + len(arrays)),
        out_specs=vmem,
        compiler_params=pltpu.CompilerParams(vmem_limit_bytes=KERNEL_VMEM),
        name="update",
    )(pieces, residual, under, *[x for x, _ in arrays])


def general(
    amplitudes,
    kept_groups,
    tile_mask,
    owner_table,
    integrals,
    residual_in,
    pair_energy,
    virt_energy,
):
    block_count = amplitudes.shape[0]
    keep_count = amplitudes.shape[1]
    pair_rows = amplitudes.shape[2]
    group_width = amplitudes.shape[3]
    column_count = integrals.shape[1]
    tile_width = group_width // tile_mask.shape[2]
    group_total = owner_table.shape[0]
    tile_keep = jnp.repeat(tile_mask.astype(amplitudes.dtype), tile_width, axis=2)
    kept_amplitudes = amplitudes * tile_keep[:, :, None, :]
    group_match = kept_groups[:, :, None] == jnp.arange(group_total, dtype=jnp.int32)[None, None, :]
    owner_slots = jnp.sum(jnp.where(group_match, owner_table[None, None, :], 0), axis=2)
    placing = owner_slots[:, None, :] == jnp.arange(group_total, dtype=jnp.int32)[None, :, None]
    outgoing = jnp.einsum(
        "bqk,bkrw->qbrw", placing.astype(jnp.bfloat16), kept_amplitudes, preferred_element_type=jnp.float32
    ).astype(jnp.bfloat16)
    full_pairs = pair_rows * lax.axis_size("virt")
    arrived = lax.all_to_all(outgoing, "pair", split_axis=0, concat_axis=0, tiled=True)
    assembled = lax.all_gather(arrived, "virt", axis=2, tiled=True)
    partial_value = jnp.dot(
        assembled.reshape(-1, group_width), integrals, preferred_element_type=jnp.float32
    )
    ladder = lax.psum_scatter(partial_value, "pair", scatter_dimension=0, tiled=True)
    denominator = pair_energy[:, None] - virt_energy[None, :]
    return (residual_in.astype(jnp.float32) + ladder) / denominator


def solution(mesh):
    sizes = dict(mesh.shape)
    regular = all(s & (s - 1) == 0 for s in sizes.values()) and sizes["pair"] <= 8
    return jax.shard_map(
        local if regular else general,
        mesh=mesh,
        in_specs=(
            P("pair", None, "virt", None),
            P("pair", None),
            P("pair", None, None),
            P(),
            P("pair", "virt"),
            P("pair", "virt"),
            P("pair"),
            P("virt"),
        ),
        out_specs=P("pair", "virt"),
        check_vma=False,
    )
```

time: 27.6 us -> 17.2 us (0.62); the launches traced: 27 us -> 17 us
  Pallas kernels: 5.59 us -> 2.08 us
  other arithmetic: 3.49 us -> 0.01 us
  waiting for transfers between devices: 7.31 us -> 5.57 us
  local copies, waits for them, and re-layouts: 1.21 us -> 0.01 us
    pallas_call x3 -> x2, Pallas kernels: 5.59 us -> 2.08 us  [the longest x1 1.09 us: prepare(): pl.pallas_call(prepare_kernel, out_shape=[jax.ShapeDtypeStruct((out_rows,...]
    concatenate x4 -> x2, other arithmetic: 2.14 us -> 0.01 us  [local(): pieces = jnp.concatenate([pieces, swap(pieces, 'virt', 1 << bit)], axis=0)]
    ppermute x6, waiting for transfers between devices: 7.31 us -> 5.57 us  [swap(): return lax.ppermute(x, axis_name, [(i, i ^ mask) for i in range(size)])]
    div x1 -> x0, other arithmetic: 1.35 us -> none  [local(): return (top + swap(far, 'pair', OUTER_BIT)) / under]
    squeeze x1 -> x0, local copies, waits for them, and re-layouts: 0.61 us -> none  [local(): far_rows = swap(pieces[1], 'pair', OUTER_BIT)]
    unnamed x4 -> x1, local copies, waits for them, and re-layouts: 0.6 us -> 0.01 us
  transfers between devices with their start and end apart: 6 -> 6, of which waited for: 4 -> 4; matrix products, arithmetic and copies ran while one was open for 8% -> 0% of each run, Pallas kernels for 7% -> 6%
where the time goes in v2:
time: 17.2 us; the launch traced here: 17 us
  starting transfers between devices  9.33 us (54%)
  waiting for transfers between devices  5.57 us (32%)
  Pallas kernels  2.08 us (12%)
    ppermute x6, starting transfers between devices, swap(): return lax.ppermute(x, axis_name, [(i, i ^ mask) for i in range(size)])  9.33 us
    ppermute x6, waiting for transfers between devices, swap(): return lax.ppermute(x, axis_name, [(i, i ^ mask) for i in range(size)])  5.57 us
    pallas_call x1, Pallas kernels, prepare(): pl.pallas_call(prepare_kernel, out_shape=[jax.ShapeDtypeStruct((out_rows,...  1.09 us
    pallas_call x1, Pallas kernels, local(): pl.pallas_call(functools.partial(update_kernel, blocks, pair_rows, [at fo...  0.99 us
  transfers between devices with their start and end apart: 6, of which 4 were waited for; matrix products, arithmetic and copies ran while one was open for 0% of the time, Pallas kernels for 6%

profile of v2, /device:TPU:0, one launch (start us, length us, event | category | flops | bytes accessed | tf_op | source)
XLA Modules:
  0.0 17.0 jit_solution(3897618797187574354)
XLA Ops:
  0.0 4.0 %collective-permute-start.2 = (bf16[1,128,256]{2,1,0:T(8,128)(2,1)}, bf16[1,128,256]{2,1,0:T(8,128)(2,1)S(1)}, u32[]{:S(2)}, u32[]{:S(2)}) collective-permute-start(bf16[1,128,256]{2,1,0:T(8,128)(2,1)} %bitcast.4), channel_id=1, source_target_pairs={{0,16},{4,20},{8,24},{12,28},{16,0},{20,4},{24,8},{28,12},{1,17},{... | collective-permute-start | bytes 196616 | tf_op jit(solution)/shard_map/ppermute | solution.py:151
  4.0 1.1 %prepare.1 = (bf16[32,128]{1,0:T(8,128)(2,1)S(1)}, bf16[1,128,256]{2,1,0:T(8,128)(2,1)S(1)}, f32[16,256]{1,0:T(8,128)S(1)}, f32[16,256]{1,0:T(8,128)S(1)}) custom-call(s32[2,4]{1,0:T(2,128)} %kept_hbm.1, s32[2,2,4]{2,1,0:T(2,128)} %bitcast.5, s32[8]{0:T(128)} %owner_hbm.1, bf16[2,4,2,128]{3,2,1,0:T(2,128)(2,1)} %amp_hbm.1, bf16[128,256]{1,0:T(8,128)(2,1)} %integrals_hbm.1, ...), custom_call_target="tpu_custom_call" | custom-call | tf_op jit(solution)/shard_map/prepare/pallas_call | solution.py:103
  5.1 0.1 collective-permute-start
  5.2 2.7 %collective-permute-done.2.refs_1_ = bf16[1,128,256]{2,1,0:T(8,128)(2,1)S(1)} collective-permute-done((bf16[1,128,256]{2,1,0:T(8,128)(2,1)}, bf16[1,128,256]{2,1,0:T(8,128)(2,1)S(1)}, u32[]{:S(2)}, u32[]{:S(2)}) %collective-permute-start.2) | collective-permute-done | bytes 65568 | tf_op jit(solution)/shard_map/ppermute | solution.py:151
  7.9 1.6 %collective-permute-start.5 = (bf16[2,128,256]{2,1,0:T(8,128)(2,1)S(1)}, bf16[2,128,256]{2,1,0:T(8,128)(2,1)S(1)}, u32[]{:S(2)}, u32[]{:S(2)}) collective-permute-start(bf16[2,128,256]{2,1,0:T(8,128)(2,1)S(1)} %constant_dynamic-update-slice_fusion), channel_id=1, source_target_pairs={{0,12},{4,8},{8,4},{12,0},{16,28},{20,24},{24,20},{28,16},{1,13},{... | collective-permute-start | bytes 393224 | tf_op jit(solution)/shard_map/ppermute | solution.py:151
  9.5 1.6 %collective-permute-start.4 = (bf16[2,128,256]{2,1,0:T(8,128)(2,1)S(1)}, bf16[2,128,256]{2,1,0:T(8,128)(2,1)S(1)}, u32[]{:S(2)}, u32[]{:S(2)}) collective-permute-start(bf16[2,128,256]{2,1,0:T(8,128)(2,1)S(1)} %constant_dynamic-update-slice_fusion), channel_id=1, source_target_pairs={{0,8},{4,12},{8,0},{12,4},{16,24},{20,28},{24,16},{28,20},{1,9},{5... | collective-permute-start | bytes 393224 | tf_op jit(solution)/shard_map/ppermute | solution.py:151
  11.1 0.3 %collective-permute-start.3 = (bf16[2,128,256]{2,1,0:T(8,128)(2,1)S(1)}, bf16[2,128,256]{2,1,0:T(8,128)(2,1)S(1)}, u32[]{:S(2)}, u32[]{:S(2)}) collective-permute-start(bf16[2,128,256]{2,1,0:T(8,128)(2,1)S(1)} %constant_dynamic-update-slice_fusion), channel_id=1, source_target_pairs={{0,4},{4,0},{8,12},{12,8},{16,20},{20,16},{24,28},{28,24},{1,5},{5... | collective-permute-start | bytes 393224 | tf_op jit(solution)/shard_map/ppermute | solution.py:151
  11.4 0.0 collective-permute-done
  11.4 1.7 %collective-permute-start.1 = (bf16[64,128]{1,0:T(8,128)(2,1)S(1)}, bf16[64,128]{1,0:T(8,128)(2,1)S(1)}, u32[]{:S(2)}, u32[]{:S(2)}) collective-permute-start(bf16[64,128]{1,0:T(8,128)(2,1)S(1)} %pad_maximum_fusion.1), channel_id=1, source_target_pairs={{0,2},{1,3},{2,0},{3,1},{4,6},{5,7},{6,4},{7,5},{8,10},{9,11},{10,... | collective-permute-start | bytes 49160 | tf_op jit(solution)/shard_map/ppermute | solution.py:151
  13.1 2.0 %collective-permute-done.1 = bf16[64,128]{1,0:T(8,128)(2,1)S(1)} collective-permute-done((bf16[64,128]{1,0:T(8,128)(2,1)S(1)}, bf16[64,128]{1,0:T(8,128)(2,1)S(1)}, u32[]{:S(2)}, u32[]{:S(2)}) %collective-permute-start.1) | collective-permute-done | bytes 16416 | tf_op jit(solution)/shard_map/ppermute | solution.py:151
  15.1 0.0 collective-permute-done.5.refs_4_
  15.1 0.4 %collective-permute-done.4.refs_3_ = bf16[2,128,256]{2,1,0:T(8,128)(2,1)S(1)} collective-permute-done((bf16[2,128,256]{2,1,0:T(8,128)(2,1)S(1)}, bf16[2,128,256]{2,1,0:T(8,128)(2,1)S(1)}, u32[]{:S(2)}, u32[]{:S(2)}) %collective-permute-start.4) | collective-permute-done | bytes 131104 | tf_op jit(solution)/shard_map/ppermute | solution.py:151
  15.6 0.5 %collective-permute-done.3.refs_2_ = bf16[2,128,256]{2,1,0:T(8,128)(2,1)S(1)} collective-permute-done((bf16[2,128,256]{2,1,0:T(8,128)(2,1)S(1)}, bf16[2,128,256]{2,1,0:T(8,128)(2,1)S(1)}, u32[]{:S(2)}, u32[]{:S(2)}) %collective-permute-start.3) | collective-permute-done | bytes 131104 | tf_op jit(solution)/shard_map/ppermute | solution.py:151
  16.0 1.0 %update.1 = f32[16,256]{1,0:T(8,128)} custom-call(bf16[128,128]{1,0:T(8,128)(2,1)S(1)} %pad_maximum_fusion.lhs_ref, f32[16,256]{1,0:T(8,128)S(1)} %get-tuple-element.10.residual_ref, f32[16,256]{1,0:T(8,128)S(1)} %get-tuple-element.11.under_ref, bf16[1,128,256]{2,1,0:T(8,128)(2,1)S(1)} %get-tuple-element.12.refs_0_, ...), custom_call_target="tpu_custom_call" | custom-call | tf_op jit(solution)/shard_map/update/pallas_call | solution.py:182
  (4 shorter events, 0.0 us)
Async XLA Ops:
  0.0 7.9 %collective-permute-start.2 = (bf16[1,128,256]{2,1,0:T(8,128)(2,1)}, bf16[1,128,256]{2,1,0:T(8,128)(2,1)S(1)}, u32[]{:S(2)}, u32[]{:S(2)}) collective-permute-start(bf16[1,128,256]{2,1,0:T(8,128)(2,1)} %bitcast.4), channel_id=1, source_target_pairs={{0,16},{4,20},{8,24},{12,28},{16,0},{20,4},{24,8},{28,12},{1,17},{... | collective-permute-start | bytes 196616 | tf_op jit(solution)/shard_map/ppermute | solution.py:151
  5.1 6.3 %collective-permute-start = (bf16[32,128]{1,0:T(8,128)(2,1)S(1)}, bf16[32,128]{1,0:T(8,128)(2,1)S(1)}, u32[]{:S(2)}, u32[]{:S(2)}) collective-permute-start(bf16[32,128]{1,0:T(8,128)(2,1)S(1)} %get-tuple-element.9), channel_id=1, source_target_pairs={{0,1},{1,0},{2,3},{3,2},{4,5},{5,4},{6,7},{7,6},{8,9},{9,8},{10,11... | collective-permute-start | bytes 24584 | tf_op jit(solution)/shard_map/ppermute | solution.py:151
  7.9 7.2 %collective-permute-start.5 = (bf16[2,128,256]{2,1,0:T(8,128)(2,1)S(1)}, bf16[2,128,256]{2,1,0:T(8,128)(2,1)S(1)}, u32[]{:S(2)}, u32[]{:S(2)}) collective-permute-start(bf16[2,128,256]{2,1,0:T(8,128)(2,1)S(1)} %constant_dynamic-update-slice_fusion), channel_id=1, source_target_pairs={{0,12},{4,8},{8,4},{12,0},{16,28},{20,24},{24,20},{28,16},{1,13},{... | collective-permute-start | bytes 393224 | tf_op jit(solution)/shard_map/ppermute | solution.py:151
  9.5 6.1 %collective-permute-start.4 = (bf16[2,128,256]{2,1,0:T(8,128)(2,1)S(1)}, bf16[2,128,256]{2,1,0:T(8,128)(2,1)S(1)}, u32[]{:S(2)}, u32[]{:S(2)}) collective-permute-start(bf16[2,128,256]{2,1,0:T(8,128)(2,1)S(1)} %constant_dynamic-update-slice_fusion), channel_id=1, source_target_pairs={{0,8},{4,12},{8,0},{12,4},{16,24},{20,28},{24,16},{28,20},{1,9},{5... | collective-permute-start | bytes 393224 | tf_op jit(solution)/shard_map/ppermute | solution.py:151
  11.1 5.0 %collective-permute-start.3 = (bf16[2,128,256]{2,1,0:T(8,128)(2,1)S(1)}, bf16[2,128,256]{2,1,0:T(8,128)(2,1)S(1)}, u32[]{:S(2)}, u32[]{:S(2)}) collective-permute-start(bf16[2,128,256]{2,1,0:T(8,128)(2,1)S(1)} %constant_dynamic-update-slice_fusion), channel_id=1, source_target_pairs={{0,4},{4,0},{8,12},{12,8},{16,20},{20,16},{24,28},{28,24},{1,5},{5... | collective-permute-start | bytes 393224 | tf_op jit(solution)/shard_map/ppermute | solution.py:151
  11.4 3.7 %collective-permute-start.1 = (bf16[64,128]{1,0:T(8,128)(2,1)S(1)}, bf16[64,128]{1,0:T(8,128)(2,1)S(1)}, u32[]{:S(2)}, u32[]{:S(2)}) collective-permute-start(bf16[64,128]{1,0:T(8,128)(2,1)S(1)} %pad_maximum_fusion.1), channel_id=1, source_target_pairs={{0,2},{1,3},{2,0},{3,1},{4,6},{5,7},{6,4},{7,5},{8,10},{9,11},{10,... | collective-permute-start | bytes 49160 | tf_op jit(solution)/shard_map/ppermute | solution.py:151

commit v3 on v2

--- a/solution.py
+++ b/solution.py
@@ -9,7 +9,6 @@
 from jax.sharding import PartitionSpec as P
 
 KERNEL_VMEM = 1 << 20
-STEPS = [(4, [0]), (1, [0, 4]), (2, [0, 4]), (3, [0, 4])]
 
 
 def prepare_kernel(
@@ -117,38 +116,39 @@
     )(*operands)
 
 
-def share_of(blocks, pair_rows, lhs, blocks_of_integrals):
-    virt_size = lhs.shape[0] // (len(blocks_of_integrals) * blocks * pair_rows)
-    full_rows = virt_size * pair_rows
-    count = len(blocks_of_integrals)
+def arrange_kernel(blocks, pair_rows, order, rows_ref, out_ref):
+    count, out_rows, _ = out_ref.shape
+    full_rows = len(order) * pair_rows
     me = lax.axis_index("virt")
-    row = lax.broadcasted_iota(jnp.int32, (blocks * full_rows, lhs.shape[0]), 0)
-    column = lax.broadcasted_iota(jnp.int32, (blocks * full_rows, lhs.shape[0]), 1)
+    row = lax.broadcasted_iota(jnp.int32, (out_rows, rows_ref.shape[0]), 0)
+    column = lax.broadcasted_iota(jnp.int32, (out_rows, rows_ref.shape[0]), 1)
     block, pair = row // full_rows, row % full_rows
-    piece = (pair // pair_rows) ^ me
-    total = None
+    apart = (pair // pair_rows) ^ me
+    piece = sum(jnp.where(apart == mask, n, 0) for n, mask in enumerate(order))
+    rows = rows_ref[...]
     for t in range(count):
         wanted = ((piece * count + t) * blocks + block) * pair_rows + pair % pair_rows
         pick = (column == wanted).astype(jnp.bfloat16)
-        left = jnp.dot(pick, lhs, preferred_element_type=jnp.float32).astype(jnp.bfloat16)
-        term = jnp.dot(left, blocks_of_integrals[t], preferred_element_type=jnp.float32)
-        total = term if total is None else total + term
-    return total
-
-
-def update_kernel(blocks, pair_rows, places, lhs_ref, residual_ref, under_ref, *refs):
+        out_ref[t] = jnp.dot(pick, rows, preferred_element_type=jnp.float32).astype(out_ref.dtype)
+
+
+def update_kernel(places, rows_ref, residual_ref, under_ref, *refs):
     *integral_refs, out_ref = refs
-    held = [None] * sum(len(p) for p in places)
+    total = residual_ref[...]
     for ref, at in zip(integral_refs, places):
         for t, place in enumerate(at):
-            held[place] = ref[t]
-    total = share_of(blocks, pair_rows, lhs_ref[...], held)
-    out_ref[...] = (residual_ref[...] + total) / under_ref[...]
-
-
-def swap(x, axis_name, mask):
-    size = lax.axis_size(axis_name)
-    return lax.ppermute(x, axis_name, [(i, i ^ mask) for i in range(size)])
+            total += jnp.dot(rows_ref[place], ref[t], preferred_element_type=jnp.float32)
+    out_ref[...] = total / under_ref[...]
+
+
+def swap(x, pair_mask, virt_mask):
+    pair_size, virt_size = lax.axis_size("pair"), lax.axis_size("virt")
+    moves = [
+        (p * virt_size + v, (p ^ pair_mask) * virt_size + (v ^ virt_mask))
+        for p in range(pair_size)
+        for v in range(virt_size)
+    ]
+    return lax.ppermute(x, ("pair", "virt"), moves)
 
 
 def local(
@@ -163,30 +163,36 @@
 ):
     blocks, _, pair_rows, _ = amplitudes.shape
     vmem = pl.BlockSpec(memory_space=pltpu.VMEM)
-    virt_bits = (lax.axis_size("virt") - 1).bit_length()
+    virt_size = lax.axis_size("virt")
     rows, own, residual, under = prepare(
         amplitudes, kept_groups, tile_mask, owner_table, integrals, residual_in, pair_energy, virt_energy
     )
-    have = {0: own}
-    arrays = [(own, (0,))]
-    for mask, labels in STEPS:
-        sent = [have[l] if (l or len(labels) > 1) else integrals[None] for l in labels]
-        sent = sent[0] if len(sent) == 1 else jnp.concatenate(sent, axis=0)
-        got = swap(sent, "pair", mask)
-        arrays.append((got, tuple(l ^ mask for l in labels)))
-        for n, l in enumerate(labels):
-            have[l ^ mask] = got if len(labels) == 1 else got[n : n + 1]
-    pieces = rows
-    for bit in range(virt_bits):
-        pieces = jnp.concatenate([pieces, swap(pieces, "virt", 1 << bit)], axis=0)
+    far = swap(integrals[None], 4, 0)
+    arrays = [(own, (0,)), (far, (4,))]
+    both = jnp.concatenate([own, far], axis=0)
+    for mask in (2, 3, 1):
+        arrays.append((swap(both, mask, 0), (mask, mask ^ 4)))
+    pieces, order = rows, [0]
+    for mask in (1, 2):
+        pieces = jnp.concatenate([pieces, swap(pieces, 0, mask)], axis=0)
+        order = order + [at ^ mask for at in order]
+    count = owner_table.shape[0]
+    slabs = pl.pallas_call(
+        functools.partial(arrange_kernel, blocks, pair_rows, order),
+        out_shape=jax.ShapeDtypeStruct((count, residual_in.shape[0], pieces.shape[1]), pieces.dtype),
+        in_specs=[vmem],
+        out_specs=vmem,
+        compiler_params=pltpu.CompilerParams(vmem_limit_bytes=KERNEL_VMEM),
+        name="arrange",
+    )(pieces)
     return pl.pallas_call(
-        functools.partial(update_kernel, blocks, pair_rows, [at for _, at in arrays]),
+        functools.partial(update_kernel, [at for _, at in arrays]),
         out_shape=jax.ShapeDtypeStruct(residual_in.shape, jnp.float32),
         in_specs=[vmem] * (3 + len(arrays)),
         out_specs=vmem,
         compiler_params=pltpu.CompilerParams(vmem_limit_bytes=KERNEL_VMEM),
         name="update",
-    )(pieces, residual, under, *[x for x, _ in arrays])
+    )(slabs, residual, under, *[x for x, _ in arrays])
 
 
 def general(

time: 17.2 us -> 16.8 us (0.977)
  waiting for transfers between devices: 5.57 us -> 5.21 us
    ppermute x6, waiting for transfers between devices: 5.57 us -> 5.21 us  [swap(): return lax.ppermute(x, ('pair', 'virt'), moves)]
    pallas_call x1 -> x2, Pallas kernels: 0.99 us -> 0.97 us  [the longest x1 0.79 us: local(): pl.pallas_call(functools.partial(update_kernel, [at for _, at in arrays])...]
  transfers between devices with their start and end apart: 6 -> 6, of which waited for: 4 -> 4; matrix products, arithmetic and copies ran while one was open for 0% -> 0% of each run, Pallas kernels for 6% -> 8%
where the time goes in v3:
time: 16.8 us; the launch traced here: 16.6 us
  starting transfers between devices  9.33 us (56%)
  waiting for transfers between devices  5.21 us (31%)
  Pallas kernels  2.06 us (12%)
    ppermute x6, starting transfers between devices, swap(): return lax.ppermute(x, ('pair', 'virt'), moves)  9.33 us
    ppermute x6, waiting for transfers between devices, swap(): return lax.ppermute(x, ('pair', 'virt'), moves)  5.21 us
    pallas_call x1, Pallas kernels, prepare(): pl.pallas_call(prepare_kernel, out_shape=[jax.ShapeDtypeStruct((out_rows,...  1.09 us
    pallas_call x1, Pallas kernels, local(): pl.pallas_call(functools.partial(update_kernel, [at for _, at in arrays])...  0.79 us
  transfers between devices with their start and end apart: 6, of which 4 were waited for; matrix products, arithmetic and copies ran while one was open for 0% of the time, Pallas kernels for 8%

profile of v3, /device:TPU:0, one launch (start us, length us, event | category | flops | bytes accessed | tf_op | source)
XLA Modules:
  0.0 16.6 jit_solution(7865698084527109293)
XLA Ops:
  0.0 4.0 %collective-permute-start.2 = (bf16[1,128,256]{2,1,0:T(8,128)(2,1)}, bf16[1,128,256]{2,1,0:T(8,128)(2,1)S(1)}, u32[]{:S(2)}, u32[]{:S(2)}) collective-permute-start(bf16[1,128,256]{2,1,0:T(8,128)(2,1)} %bitcast.4), channel_id=1, source_target_pairs={{0,16},{1,17},{2,18},{3,19},{4,20},{5,21},{6,22},{7,23},{8,24},{9,... | collective-permute-start | bytes 196616 | tf_op jit(solution)/shard_map/ppermute | solution.py:151
  4.0 1.1 %prepare.1 = (bf16[32,128]{1,0:T(8,128)(2,1)S(1)}, bf16[1,128,256]{2,1,0:T(8,128)(2,1)S(1)}, f32[16,256]{1,0:T(8,128)S(1)}, f32[16,256]{1,0:T(8,128)S(1)}) custom-call(s32[2,4]{1,0:T(2,128)} %kept_hbm.1, s32[2,2,4]{2,1,0:T(2,128)} %bitcast.5, s32[8]{0:T(128)} %owner_hbm.1, bf16[2,4,2,128]{3,2,1,0:T(2,128)(2,1)} %amp_hbm.1, bf16[128,256]{1,0:T(8,128)(2,1)} %integrals_hbm.1, ...), custom_call_target="tpu_custom_call" | custom-call | tf_op jit(solution)/shard_map/prepare/pallas_call | solution.py:102
  5.1 0.1 collective-permute-start
  5.2 2.7 %collective-permute-done.2.refs_1_ = bf16[1,128,256]{2,1,0:T(8,128)(2,1)S(1)} collective-permute-done((bf16[1,128,256]{2,1,0:T(8,128)(2,1)}, bf16[1,128,256]{2,1,0:T(8,128)(2,1)S(1)}, u32[]{:S(2)}, u32[]{:S(2)}) %collective-permute-start.2) | collective-permute-done | bytes 65568 | tf_op jit(solution)/shard_map/ppermute | solution.py:151
  7.9 1.7 %collective-permute-start.5 = (bf16[2,128,256]{2,1,0:T(8,128)(2,1)S(1)}, bf16[2,128,256]{2,1,0:T(8,128)(2,1)S(1)}, u32[]{:S(2)}, u32[]{:S(2)}) collective-permute-start(bf16[2,128,256]{2,1,0:T(8,128)(2,1)S(1)} %constant_dynamic-update-slice_fusion), channel_id=1, source_target_pairs={{0,4},{1,5},{2,6},{3,7},{4,0},{5,1},{6,2},{7,3},{8,12},{9,13},{10,... | collective-permute-start | bytes 393224 | tf_op jit(solution)/shard_map/ppermute | solution.py:151
  9.6 0.4 %collective-permute-start.4 = (bf16[2,128,256]{2,1,0:T(8,128)(2,1)S(1)}, bf16[2,128,256]{2,1,0:T(8,128)(2,1)S(1)}, u32[]{:S(2)}, u32[]{:S(2)}) collective-permute-start(bf16[2,128,256]{2,1,0:T(8,128)(2,1)S(1)} %constant_dynamic-update-slice_fusion), channel_id=1, source_target_pairs={{0,12},{1,13},{2,14},{3,15},{4,8},{5,9},{6,10},{7,11},{8,4},{9,5},... | collective-permute-start | bytes 393224 | tf_op jit(solution)/shard_map/ppermute | solution.py:151
  10.0 1.3 %collective-permute-start.3 = (bf16[2,128,256]{2,1,0:T(8,128)(2,1)S(1)}, bf16[2,128,256]{2,1,0:T(8,128)(2,1)S(1)}, u32[]{:S(2)}, u32[]{:S(2)}) collective-permute-start(bf16[2,128,256]{2,1,0:T(8,128)(2,1)S(1)} %constant_dynamic-update-slice_fusion), channel_id=1, source_target_pairs={{0,8},{1,9},{2,10},{3,11},{4,12},{5,13},{6,14},{7,15},{8,0},{9,1},... | collective-permute-start | bytes 393224 | tf_op jit(solution)/shard_map/ppermute | solution.py:151
  11.4 0.0 collective-permute-done
  11.4 1.7 %collective-permute-start.1 = (bf16[64,128]{1,0:T(8,128)(2,1)S(1)}, bf16[64,128]{1,0:T(8,128)(2,1)S(1)}, u32[]{:S(2)}, u32[]{:S(2)}) collective-permute-start(bf16[64,128]{1,0:T(8,128)(2,1)S(1)} %pad_maximum_fusion.1), channel_id=1, source_target_pairs={{0,2},{1,3},{2,0},{3,1},{4,6},{5,7},{6,4},{7,5},{8,10},{9,11},{10,... | collective-permute-start | bytes 49160 | tf_op jit(solution)/shard_map/ppermute | solution.py:151
  13.1 2.0 %collective-permute-done.1 = bf16[64,128]{1,0:T(8,128)(2,1)S(1)} collective-permute-done((bf16[64,128]{1,0:T(8,128)(2,1)S(1)}, bf16[64,128]{1,0:T(8,128)(2,1)S(1)}, u32[]{:S(2)}, u32[]{:S(2)}) %collective-permute-start.1) | collective-permute-done | bytes 16416 | tf_op jit(solution)/shard_map/ppermute | solution.py:151
  15.1 0.2 %arrange.1.rows_ref = bf16[8,16,128]{2,1,0:T(8,128)(2,1)S(1)} custom-call(bf16[128,128]{1,0:T(8,128)(2,1)S(1)} %pad_maximum_fusion.rows_ref), custom_call_target="tpu_custom_call" | custom-call | tf_op jit(solution)/shard_map/arrange/pallas_call | solution.py:180
  15.3 0.0 collective-permute-done.5.refs_4_
  15.3 0.1 collective-permute-done.4.refs_3_
  15.5 0.4 %collective-permute-done.3.refs_2_ = bf16[2,128,256]{2,1,0:T(8,128)(2,1)S(1)} collective-permute-done((bf16[2,128,256]{2,1,0:T(8,128)(2,1)S(1)}, bf16[2,128,256]{2,1,0:T(8,128)(2,1)S(1)}, u32[]{:S(2)}, u32[]{:S(2)}) %collective-permute-start.3) | collective-permute-done | bytes 131104 | tf_op jit(solution)/shard_map/ppermute | solution.py:151
  15.9 0.8 %update.1 = f32[16,256]{1,0:T(8,128)} custom-call(bf16[8,16,128]{2,1,0:T(8,128)(2,1)S(1)} %arrange.1.rows_ref, f32[16,256]{1,0:T(8,128)S(1)} %get-tuple-element.10.residual_ref, f32[16,256]{1,0:T(8,128)S(1)} %get-tuple-element.11.under_ref, bf16[1,128,256]{2,1,0:T(8,128)(2,1)S(1)} %get-tuple-element.12.refs_0_, ...), custom_call_target="tpu_custom_call" | custom-call | tf_op jit(solution)/shard_map/update/pallas_call | solution.py:188
  (4 shorter events, 0.0 us)
Async XLA Ops:
  0.0 7.9 %collective-permute-start.2 = (bf16[1,128,256]{2,1,0:T(8,128)(2,1)}, bf16[1,128,256]{2,1,0:T(8,128)(2,1)S(1)}, u32[]{:S(2)}, u32[]{:S(2)}) collective-permute-start(bf16[1,128,256]{2,1,0:T(8,128)(2,1)} %bitcast.4), channel_id=1, source_target_pairs={{0,16},{1,17},{2,18},{3,19},{4,20},{5,21},{6,22},{7,23},{8,24},{9,... | collective-permute-start | bytes 196616 | tf_op jit(solution)/shard_map/ppermute | solution.py:151
  5.1 6.3 %collective-permute-start = (bf16[32,128]{1,0:T(8,128)(2,1)S(1)}, bf16[32,128]{1,0:T(8,128)(2,1)S(1)}, u32[]{:S(2)}, u32[]{:S(2)}) collective-permute-start(bf16[32,128]{1,0:T(8,128)(2,1)S(1)} %get-tuple-element.9), channel_id=1, source_target_pairs={{0,1},{1,0},{2,3},{3,2},{4,5},{5,4},{6,7},{7,6},{8,9},{9,8},{10,11... | collective-permute-start | bytes 24584 | tf_op jit(solution)/shard_map/ppermute | solution.py:151
  7.9 7.4 %collective-permute-start.5 = (bf16[2,128,256]{2,1,0:T(8,128)(2,1)S(1)}, bf16[2,128,256]{2,1,0:T(8,128)(2,1)S(1)}, u32[]{:S(2)}, u32[]{:S(2)}) collective-permute-start(bf16[2,128,256]{2,1,0:T(8,128)(2,1)S(1)} %constant_dynamic-update-slice_fusion), channel_id=1, source_target_pairs={{0,4},{1,5},{2,6},{3,7},{4,0},{5,1},{6,2},{7,3},{8,12},{9,13},{10,... | collective-permute-start | bytes 393224 | tf_op jit(solution)/shard_map/ppermute | solution.py:151
  9.6 5.9 %collective-permute-start.4 = (bf16[2,128,256]{2,1,0:T(8,128)(2,1)S(1)}, bf16[2,128,256]{2,1,0:T(8,128)(2,1)S(1)}, u32[]{:S(2)}, u32[]{:S(2)}) collective-permute-start(bf16[2,128,256]{2,1,0:T(8,128)(2,1)S(1)} %constant_dynamic-update-slice_fusion), channel_id=1, source_target_pairs={{0,12},{1,13},{2,14},{3,15},{4,8},{5,9},{6,10},{7,11},{8,4},{9,5},... | collective-permute-start | bytes 393224 | tf_op jit(solution)/shard_map/ppermute | solution.py:151
  10.0 5.8 %collective-permute-start.3 = (bf16[2,128,256]{2,1,0:T(8,128)(2,1)S(1)}, bf16[2,128,256]{2,1,0:T(8,128)(2,1)S(1)}, u32[]{:S(2)}, u32[]{:S(2)}) collective-permute-start(bf16[2,128,256]{2,1,0:T(8,128)(2,1)S(1)} %constant_dynamic-update-slice_fusion), channel_id=1, source_target_pairs={{0,8},{1,9},{2,10},{3,11},{4,12},{5,13},{6,14},{7,15},{8,0},{9,1},... | collective-permute-start | bytes 393224 | tf_op jit(solution)/shard_map/ppermute | solution.py:151
  11.4 3.7 %collective-permute-start.1 = (bf16[64,128]{1,0:T(8,128)(2,1)S(1)}, bf16[64,128]{1,0:T(8,128)(2,1)S(1)}, u32[]{:S(2)}, u32[]{:S(2)}) collective-permute-start(bf16[64,128]{1,0:T(8,128)(2,1)S(1)} %pad_maximum_fusion.1), channel_id=1, source_target_pairs={{0,2},{1,3},{2,0},{3,1},{4,6},{5,7},{6,4},{7,5},{8,10},{9,11},{10,... | collective-permute-start | bytes 49160 | tf_op jit(solution)/shard_map/ppermute | solution.py:151

commit v4 on v3

--- a/solution.py
+++ b/solution.py
@@ -1,5 +1,4 @@
 import functools
-import math
 
 import jax
 import jax.numpy as jnp
@@ -53,13 +52,14 @@
         move.start()
     blocks, keep, pair_rows, width = amp_ref.shape
     tiles = mask_ref.shape[1]
+    tasks = blocks * keep
+    own_rows = rows_ref.shape[1]
+    count = rows_ref.shape[2] // width
     me = lax.axis_index("pair")
     lane_tile = lax.broadcasted_iota(jnp.int32, (pair_rows, width), 1) // (width // tiles)
-    out_rows = rows_ref.shape[0]
-    tasks = blocks * keep
-    row = lax.broadcasted_iota(jnp.int32, (out_rows, tasks * pair_rows), 0)
-    column = lax.broadcasted_iota(jnp.int32, (out_rows, tasks * pair_rows), 1)
-    wanted = jnp.full((out_rows, tasks * pair_rows), -1, jnp.int32)
+    row = lax.broadcasted_iota(jnp.int32, (count * own_rows, tasks * pair_rows), 0)
+    column = lax.broadcasted_iota(jnp.int32, (count * own_rows, tasks * pair_rows), 1)
+    wanted = jnp.full(row.shape, -1, jnp.int32)
     for move in moves:
         move.wait()
     for b in range(blocks):
@@ -72,9 +72,9 @@
                 scale = jnp.where(lane_tile == s, mask_ref[b, s, k].astype(jnp.float32), scale)
             kept_rows_ref[pl.ds(task * pair_rows, pair_rows), :] = amp_ref[b, k].astype(jnp.float32) * scale
     pick = (row == wanted).astype(jnp.bfloat16)
-    rows_ref[...] = jnp.dot(
-        pick, kept_rows_ref[...].astype(jnp.bfloat16), preferred_element_type=jnp.float32
-    ).astype(rows_ref.dtype)
+    spread = jnp.dot(pick, kept_rows_ref[...].astype(jnp.bfloat16), preferred_element_type=jnp.float32)
+    for t in range(count):
+        rows_ref[0, :, t * width : (t + 1) * width] = spread[t * own_rows : (t + 1) * own_rows].astype(rows_ref.dtype)
     residual_ref[...] = rest_ref[...].astype(jnp.float32)
     count = under_ref.shape[0]
     here = lax.broadcasted_iota(jnp.int32, (count, count), 0)
@@ -85,7 +85,7 @@
 
 def prepare(amplitudes, kept_groups, tile_mask, owner_table, integrals, residual_in, pair_energy, virt_energy):
     blocks, keep, pair_rows, width = amplitudes.shape
-    out_rows = owner_table.shape[0] * blocks * pair_rows
+    rows_shape = (1, blocks * pair_rows, owner_table.shape[0] * width)
     operands = (
         kept_groups,
         jnp.swapaxes(tile_mask, 1, 2),
@@ -102,7 +102,7 @@
     return pl.pallas_call(
         prepare_kernel,
         out_shape=[
-            jax.ShapeDtypeStruct((out_rows, width), amplitudes.dtype),
+            jax.ShapeDtypeStruct(rows_shape, amplitudes.dtype),
             jax.ShapeDtypeStruct((1, *integrals.shape), integrals.dtype),
             jax.ShapeDtypeStruct(residual_in.shape, jnp.float32),
             jax.ShapeDtypeStruct(residual_in.shape, jnp.float32),
@@ -116,28 +116,29 @@
     )(*operands)
 
 
-def arrange_kernel(blocks, pair_rows, order, rows_ref, out_ref):
-    count, out_rows, _ = out_ref.shape
+def update_kernel(
+    blocks, pair_rows, order, places, first_ref, more_ref, residual_ref, under_ref, *refs
+):
+    *integral_refs, out_ref, sorted_ref, rows_ref = refs
+    width = integral_refs[0].shape[1]
     full_rows = len(order) * pair_rows
     me = lax.axis_index("virt")
-    row = lax.broadcasted_iota(jnp.int32, (out_rows, rows_ref.shape[0]), 0)
-    column = lax.broadcasted_iota(jnp.int32, (out_rows, rows_ref.shape[0]), 1)
-    block, pair = row // full_rows, row % full_rows
-    apart = (pair // pair_rows) ^ me
-    piece = sum(jnp.where(apart == mask, n, 0) for n, mask in enumerate(order))
-    rows = rows_ref[...]
-    for t in range(count):
-        wanted = ((piece * count + t) * blocks + block) * pair_rows + pair % pair_rows
-        pick = (column == wanted).astype(jnp.bfloat16)
-        out_ref[t] = jnp.dot(pick, rows, preferred_element_type=jnp.float32).astype(out_ref.dtype)
-
-
-def update_kernel(places, rows_ref, residual_ref, under_ref, *refs):
-    *integral_refs, out_ref = refs
+    pieces = [first_ref[n] for n in range(first_ref.shape[0])]
+    pieces += [more_ref[n] for n in range(more_ref.shape[0])]
+    for mask, piece in zip(order, pieces):
+        sorted_ref[me ^ mask] = piece.astype(jnp.float32)
+    for v in range(len(order)):
+        for b in range(blocks):
+            rows_ref[pl.ds(b * full_rows + v * pair_rows, pair_rows), :] = sorted_ref[
+                v, pl.ds(b * pair_rows, pair_rows), :
+            ]
+    rows = rows_ref[...].astype(jnp.bfloat16)
     total = residual_ref[...]
     for ref, at in zip(integral_refs, places):
-        for t, place in enumerate(at):
-            total += jnp.dot(rows_ref[place], ref[t], preferred_element_type=jnp.float32)
+        for n, place in enumerate(at):
+            total += jnp.dot(
+                rows[:, place * width : (place + 1) * width], ref[n], preferred_element_type=jnp.float32
+            )
     out_ref[...] = total / under_ref[...]
 
 
@@ -164,35 +165,35 @@
     blocks, _, pair_rows, _ = amplitudes.shape
     vmem = pl.BlockSpec(memory_space=pltpu.VMEM)
     virt_size = lax.axis_size("virt")
+
+    diagonal = swap(integrals[None], 3, 0)
+    far = swap(integrals[None], 4, 0)
+
     rows, own, residual, under = prepare(
         amplitudes, kept_groups, tile_mask, owner_table, integrals, residual_in, pair_energy, virt_energy
     )
-    far = swap(integrals[None], 4, 0)
-    arrays = [(own, (0,)), (far, (4,))]
+    pieces, order, more = rows, [0], None
+    for bit in range((virt_size - 1).bit_length()):
+        if more is not None:
+            pieces = jnp.concatenate([pieces, more], axis=0)
+        more = swap(pieces, 0, 1 << bit)
+        order = order + [at ^ (1 << bit) for at in order]
+
     both = jnp.concatenate([own, far], axis=0)
-    for mask in (2, 3, 1):
-        arrays.append((swap(both, mask, 0), (mask, mask ^ 4)))
-    pieces, order = rows, [0]
-    for mask in (1, 2):
-        pieces = jnp.concatenate([pieces, swap(pieces, 0, mask)], axis=0)
-        order = order + [at ^ mask for at in order]
-    count = owner_table.shape[0]
-    slabs = pl.pallas_call(
-        functools.partial(arrange_kernel, blocks, pair_rows, order),
-        out_shape=jax.ShapeDtypeStruct((count, residual_in.shape[0], pieces.shape[1]), pieces.dtype),
-        in_specs=[vmem],
+    arrays = [(own, (0,)), (diagonal, (3,)), (far, (4,)), (swap(far, 3, 0), (7,))]
+    arrays += [(swap(both, mask, 0), (mask, mask ^ 4)) for mask in (2, 1)]
+    return pl.pallas_call(
+        functools.partial(update_kernel, blocks, pair_rows, order, [at for _, at in arrays]),
+        out_shape=jax.ShapeDtypeStruct(residual_in.shape, jnp.float32),
+        in_specs=[vmem] * (4 + len(arrays)),
         out_specs=vmem,
-        compiler_params=pltpu.CompilerParams(vmem_limit_bytes=KERNEL_VMEM),
-        name="arrange",
-    )(pieces)
-    return pl.pallas_call(
-        functools.partial(update_kernel, [at for _, at in arrays]),
-        out_shape=jax.ShapeDtypeStruct(residual_in.shape, jnp.float32),
-        in_specs=[vmem] * (3 + len(arrays)),
-        out_specs=vmem,
+        scratch_shapes=[
+            pltpu.VMEM((virt_size, *pieces.shape[1:]), jnp.float32),
+            pltpu.VMEM((residual_in.shape[0], pieces.shape[2]), jnp.float32),
+        ],
         compiler_params=pltpu.CompilerParams(vmem_limit_bytes=KERNEL_VMEM),
         name="update",
-    )(slabs, residual, under, *[x for x, _ in arrays])
+    )(pieces, more, residual, under, *[x for x, _ in arrays])
 
 
 def general(
@@ -232,8 +233,8 @@
 
 
 def solution(mesh):
-    sizes = dict(mesh.shape)
-    regular = all(s & (s - 1) == 0 for s in sizes.values()) and sizes["pair"] <= 8
+    pair_size, virt_size = mesh.shape["pair"], mesh.shape["virt"]
+    regular = pair_size == 8 and virt_size in (2, 4, 8)
     return jax.shard_map(
         local if regular else general,
         mesh=mesh,

time: 16.8 us -> 16.3 us (0.970)
  waiting for transfers between devices: 5.21 us -> 2.42 us
  starting transfers between devices: 9.33 us -> 11.7 us
    ppermute x6 -> x7, waiting for transfers between devices: 5.21 us -> 2.42 us  [swap(): return lax.ppermute(x, ('pair', 'virt'), moves)]
    ppermute x6 -> x7, starting transfers between devices: 9.33 us -> 11.7 us  [swap(): return lax.ppermute(x, ('pair', 'virt'), moves)]
    pallas_call x3 -> x2, Pallas kernels: 2.06 us -> 1.91 us  [the longest x1 1.1 us: prepare(): pl.pallas_call(prepare_kernel, out_shape=[jax.ShapeDtypeStruct(rows_shape...]
  transfers between devices with their start and end apart: 6 -> 7, of which waited for: 4 -> 2; matrix products, arithmetic and copies ran while one was open for 0% -> 0% of each run, Pallas kernels for 8% -> 7%
where the time goes in v4:
time: 16.3 us; the launch traced here: 16.2 us
  starting transfers between devices  11.7 us (72%)
  waiting for transfers between devices  2.42 us (15%)
  Pallas kernels  1.91 us (12%)
    ppermute x7, starting transfers between devices, swap(): return lax.ppermute(x, ('pair', 'virt'), moves)  11.7 us
    ppermute x7, waiting for transfers between devices, swap(): return lax.ppermute(x, ('pair', 'virt'), moves)  2.42 us
    pallas_call x1, Pallas kernels, prepare(): pl.pallas_call(prepare_kernel, out_shape=[jax.ShapeDtypeStruct(rows_shape...  1.1 us
    pallas_call x1, Pallas kernels, local(): pl.pallas_call(functools.partial(update_kernel, blocks, pair_rows, order,...  0.82 us
  transfers between devices with their start and end apart: 7, of which 2 were waited for; matrix products, arithmetic and copies ran while one was open for 0% of the time, Pallas kernels for 7%

profile of v4, /device:TPU:0, one launch (start us, length us, event | category | flops | bytes accessed | tf_op | source)
XLA Modules:
  0.0 16.2 jit_solution(1778659048691676569)
XLA Ops:
  0.0 4.0 %collective-permute-start.3 = (bf16[1,128,256]{2,1,0:T(8,128)(2,1)}, bf16[1,128,256]{2,1,0:T(8,128)(2,1)S(1)}, u32[]{:S(2)}, u32[]{:S(2)}) collective-permute-start(bf16[1,128,256]{2,1,0:T(8,128)(2,1)} %bitcast.4), channel_id=1, source_target_pairs={{0,16},{1,17},{2,18},{3,19},{4,20},{5,21},{6,22},{7,23},{8,24},{9,... | collective-permute-start | bytes 196616 | tf_op jit(solution)/shard_map/ppermute | solution.py:152
  4.0 2.5 %collective-permute-start.2 = (bf16[1,128,256]{2,1,0:T(8,128)(2,1)}, bf16[1,128,256]{2,1,0:T(8,128)(2,1)S(1)}, u32[]{:S(2)}, u32[]{:S(2)}) collective-permute-start(bf16[1,128,256]{2,1,0:T(8,128)(2,1)} %bitcast.5), channel_id=1, source_target_pairs={{0,12},{1,13},{2,14},{3,15},{4,8},{5,9},{6,10},{7,11},{8,4},{9,5},... | collective-permute-start | bytes 196616 | tf_op jit(solution)/shard_map/ppermute | solution.py:152
  6.5 1.1 %prepare.1 = (bf16[1,4,1024]{2,1,0:T(4,128)(2,1)S(1)}, bf16[1,128,256]{2,1,0:T(8,128)(2,1)S(1)}, f32[16,256]{1,0:T(8,128)S(1)}, f32[16,256]{1,0:T(8,128)S(1)}) custom-call(s32[2,4]{1,0:T(2,128)} %kept_hbm.1, s32[2,2,4]{2,1,0:T(2,128)} %bitcast.6, s32[8]{0:T(128)} %owner_hbm.1, bf16[2,4,2,128]{3,2,1,0:T(2,128)(2,1)} %amp_hbm.1, ...), custom_call_target="tpu_custom_call" | custom-call | tf_op jit(solution)/shard_map/prepare/pallas_call | solution.py:102
  7.6 0.1 collective-permute-start
  7.7 0.0 collective-permute-done.3.refs_2_
  7.8 1.3 %collective-permute-start.5 = (bf16[2,128,256]{2,1,0:T(8,128)(2,1)S(1)}, bf16[2,128,256]{2,1,0:T(8,128)(2,1)S(1)}, u32[]{:S(2)}, u32[]{:S(2)}) collective-permute-start(bf16[2,128,256]{2,1,0:T(8,128)(2,1)S(1)} %constant_dynamic-update-slice_fusion.2), channel_id=1, source_target_pairs={{0,8},{1,9},{2,10},{3,11},{4,12},{5,13},{6,14},{7,15},{8,0},{9,1},... | collective-permute-start | bytes 393224 | tf_op jit(solution)/shard_map/ppermute | solution.py:152
  9.1 1.1 %collective-permute-start.6 = (bf16[2,128,256]{2,1,0:T(8,128)(2,1)S(1)}, bf16[2,128,256]{2,1,0:T(8,128)(2,1)S(1)}, u32[]{:S(2)}, u32[]{:S(2)}) collective-permute-start(bf16[2,128,256]{2,1,0:T(8,128)(2,1)S(1)} %constant_dynamic-update-slice_fusion.2), channel_id=1, source_target_pairs={{0,4},{1,5},{2,6},{3,7},{4,0},{5,1},{6,2},{7,3},{8,12},{9,13},{10,... | collective-permute-start | bytes 393224 | tf_op jit(solution)/shard_map/ppermute | solution.py:152
  10.2 1.2 %collective-permute-start.4 = (bf16[1,128,256]{2,1,0:T(8,128)(2,1)S(1)}, bf16[1,128,256]{2,1,0:T(8,128)(2,1)S(1)}, u32[]{:S(2)}, u32[]{:S(2)}) collective-permute-start(bf16[1,128,256]{2,1,0:T(8,128)(2,1)S(1)} %collective-permute-done.3.refs_2_), channel_id=1, source_target_pairs={{0,12},{1,13},{2,14},{3,15},{4,8},{5,9},{6,10},{7,11},{8,4},{9,5},... | collective-permute-start | bytes 196616 | tf_op jit(solution)/shard_map/ppermute | solution.py:152
  11.3 0.0 collective-permute-done
  11.3 1.6 %collective-permute-start.1 = (bf16[2,4,1024]{2,1,0:T(4,128)(2,1)S(1)}, bf16[2,4,1024]{2,1,0:T(4,128)(2,1)S(1)}, u32[]{:S(2)}, u32[]{:S(2)}) collective-permute-start(bf16[2,4,1024]{2,1,0:T(4,128)(2,1)S(1)} %constant_dynamic-update-slice_fusion.first_ref), channel_id=1, source_target_pairs={{0,2},{1,3},{2,0},{3,1},{4,6},{5,7},{6,4},{7,5},{8,10},{9,11},{10,... | collective-permute-start | bytes 49160 | tf_op jit(solution)/shard_map/ppermute | solution.py:152
  12.9 2.2 %collective-permute-done.1.more_ref = bf16[2,4,1024]{2,1,0:T(4,128)(2,1)S(1)} collective-permute-done((bf16[2,4,1024]{2,1,0:T(4,128)(2,1)S(1)}, bf16[2,4,1024]{2,1,0:T(4,128)(2,1)S(1)}, u32[]{:S(2)}, u32[]{:S(2)}) %collective-permute-start.1) | collective-permute-done | bytes 16416 | tf_op jit(solution)/shard_map/ppermute | solution.py:152
  15.1 0.0 collective-permute-done.2.refs_1_
  15.1 0.2 %collective-permute-done.4.refs_3_ = bf16[1,128,256]{2,1,0:T(8,128)(2,1)S(1)} collective-permute-done((bf16[1,128,256]{2,1,0:T(8,128)(2,1)S(1)}, bf16[1,128,256]{2,1,0:T(8,128)(2,1)S(1)}, u32[]{:S(2)}, u32[]{:S(2)}) %collective-permute-start.4) | collective-permute-done | bytes 65568 | tf_op jit(solution)/shard_map/ppermute | solution.py:152
  15.3 0.0 collective-permute-done.5.refs_4_
  15.3 0.0 collective-permute-done.6.refs_5_
  15.3 0.8 %update.1 = f32[16,256]{1,0:T(8,128)} custom-call(bf16[2,4,1024]{2,1,0:T(4,128)(2,1)S(1)} %constant_dynamic-update-slice_fusion.first_ref, bf16[2,4,1024]{2,1,0:T(4,128)(2,1)S(1)} %collective-permute-done.1.more_ref, f32[16,256]{1,0:T(8,128)S(1)} %get-tuple-element.10.residual_ref, f32[16,256]{1,0:T(8,128)S(1)} %get-tuple-element.11.under_ref, ...), custom_call_target="tpu_custom_call" | custom-call | tf_op jit(solution)/shard_map/update/pallas_call | solution.py:185
  (4 shorter events, 0.0 us)
Async XLA Ops:
  0.0 7.7 %collective-permute-start.3 = (bf16[1,128,256]{2,1,0:T(8,128)(2,1)}, bf16[1,128,256]{2,1,0:T(8,128)(2,1)S(1)}, u32[]{:S(2)}, u32[]{:S(2)}) collective-permute-start(bf16[1,128,256]{2,1,0:T(8,128)(2,1)} %bitcast.4), channel_id=1, source_target_pairs={{0,16},{1,17},{2,18},{3,19},{4,20},{5,21},{6,22},{7,23},{8,24},{9,... | collective-permute-start | bytes 196616 | tf_op jit(solution)/shard_map/ppermute | solution.py:152
  4.0 11.1 %collective-permute-start.2 = (bf16[1,128,256]{2,1,0:T(8,128)(2,1)}, bf16[1,128,256]{2,1,0:T(8,128)(2,1)S(1)}, u32[]{:S(2)}, u32[]{:S(2)}) collective-permute-start(bf16[1,128,256]{2,1,0:T(8,128)(2,1)} %bitcast.5), channel_id=1, source_target_pairs={{0,12},{1,13},{2,14},{3,15},{4,8},{5,9},{6,10},{7,11},{8,4},{9,5},... | collective-permute-start | bytes 196616 | tf_op jit(solution)/shard_map/ppermute | solution.py:152
  7.6 3.7 %collective-permute-start = (bf16[1,4,1024]{2,1,0:T(4,128)(2,1)S(1)}, bf16[1,4,1024]{2,1,0:T(4,128)(2,1)S(1)}, u32[]{:S(2)}, u32[]{:S(2)}) collective-permute-start(bf16[1,4,1024]{2,1,0:T(4,128)(2,1)S(1)} %get-tuple-element.9), channel_id=1, source_target_pairs={{0,1},{1,0},{2,3},{3,2},{4,5},{5,4},{6,7},{7,6},{8,9},{9,8},{10,11... | collective-permute-start | bytes 24584 | tf_op jit(solution)/shard_map/ppermute | solution.py:152
  7.8 7.6 %collective-permute-start.5 = (bf16[2,128,256]{2,1,0:T(8,128)(2,1)S(1)}, bf16[2,128,256]{2,1,0:T(8,128)(2,1)S(1)}, u32[]{:S(2)}, u32[]{:S(2)}) collective-permute-start(bf16[2,128,256]{2,1,0:T(8,128)(2,1)S(1)} %constant_dynamic-update-slice_fusion.2), channel_id=1, source_target_pairs={{0,8},{1,9},{2,10},{3,11},{4,12},{5,13},{6,14},{7,15},{8,0},{9,1},... | collective-permute-start | bytes 393224 | tf_op jit(solution)/shard_map/ppermute | solution.py:152
  9.1 6.3 %collective-permute-start.6 = (bf16[2,128,256]{2,1,0:T(8,128)(2,1)S(1)}, bf16[2,128,256]{2,1,0:T(8,128)(2,1)S(1)}, u32[]{:S(2)}, u32[]{:S(2)}) collective-permute-start(bf16[2,128,256]{2,1,0:T(8,128)(2,1)S(1)} %constant_dynamic-update-slice_fusion.2), channel_id=1, source_target_pairs={{0,4},{1,5},{2,6},{3,7},{4,0},{5,1},{6,2},{7,3},{8,12},{9,13},{10,... | collective-permute-start | bytes 393224 | tf_op jit(solution)/shard_map/ppermute | solution.py:152
  10.2 5.2 %collective-permute-start.4 = (bf16[1,128,256]{2,1,0:T(8,128)(2,1)S(1)}, bf16[1,128,256]{2,1,0:T(8,128)(2,1)S(1)}, u32[]{:S(2)}, u32[]{:S(2)}) collective-permute-start(bf16[1,128,256]{2,1,0:T(8,128)(2,1)S(1)} %collective-permute-done.3.refs_2_), channel_id=1, source_target_pairs={{0,12},{1,13},{2,14},{3,15},{4,8},{5,9},{6,10},{7,11},{8,4},{9,5},... | collective-permute-start | bytes 196616 | tf_op jit(solution)/shard_map/ppermute | solution.py:152
  11.3 3.8 %collective-permute-start.1 = (bf16[2,4,1024]{2,1,0:T(4,128)(2,1)S(1)}, bf16[2,4,1024]{2,1,0:T(4,128)(2,1)S(1)}, u32[]{:S(2)}, u32[]{:S(2)}) collective-permute-start(bf16[2,4,1024]{2,1,0:T(4,128)(2,1)S(1)} %constant_dynamic-update-slice_fusion.first_ref), channel_id=1, source_target_pairs={{0,2},{1,3},{2,0},{3,1},{4,6},{5,7},{6,4},{7,5},{8,10},{9,11},{10,... | collective-permute-start | bytes 49160 | tf_op jit(solution)/shard_map/ppermute | solution.py:152

commit v5 on v4

--- a/solution.py
+++ b/solution.py
@@ -117,9 +117,9 @@
 
 
 def update_kernel(
-    blocks, pair_rows, order, places, first_ref, more_ref, residual_ref, under_ref, *refs
-):
-    *integral_refs, out_ref, sorted_ref, rows_ref = refs
+    blocks, pair_rows, order, places, *refs
+):
+    *integral_refs, first_ref, more_ref, residual_ref, under_ref, out_ref, sorted_ref, rows_ref = refs
     width = integral_refs[0].shape[1]
     full_rows = len(order) * pair_rows
     me = lax.axis_index("virt")
@@ -176,12 +176,15 @@
     for bit in range((virt_size - 1).bit_length()):
         if more is not None:
             pieces = jnp.concatenate([pieces, more], axis=0)
-        more = swap(pieces, 0, 1 << bit)
-        order = order + [at ^ (1 << bit) for at in order]
+        mask = (1 << bit) | 1
+        more = swap(pieces, 0, mask)
+        order = order + [at ^ mask for at in order]
 
     both = jnp.concatenate([own, far], axis=0)
-    arrays = [(own, (0,)), (diagonal, (3,)), (far, (4,)), (swap(far, 3, 0), (7,))]
-    arrays += [(swap(both, mask, 0), (mask, mask ^ 4)) for mask in (2, 1)]
+    along_x = swap(both, 1, 0)
+    beyond = swap(far, 3, 0)
+    along_z = swap(both, 2, 0)
+    arrays = [(along_z, (2, 6)), (own, (0,)), (diagonal, (3,)), (far, (4,)), (beyond, (7,)), (along_x, (1, 5))]
     return pl.pallas_call(
         functools.partial(update_kernel, blocks, pair_rows, order, [at for _, at in arrays]),
         out_shape=jax.ShapeDtypeStruct(residual_in.shape, jnp.float32),
@@ -193,7 +196,7 @@
         ],
         compiler_params=pltpu.CompilerParams(vmem_limit_bytes=KERNEL_VMEM),
         name="update",
-    )(pieces, more, residual, under, *[x for x, _ in arrays])
+    )(*[x for x, _ in arrays], pieces, more, residual, under)
 
 
 def general(

time: 16.3 us -> 16.3 us (level)
  waiting for transfers between devices: 2.42 us -> 3.17 us
  starting transfers between devices: 11.7 us -> 11 us
    ppermute x7, starting transfers between devices: 11.7 us -> 11 us  [swap(): return lax.ppermute(x, ('pair', 'virt'), moves)]
    ppermute x7, waiting for transfers between devices: 2.42 us -> 3.17 us  [swap(): return lax.ppermute(x, ('pair', 'virt'), moves)]
where the time goes in v5:
time: 16.3 us; the launch traced here: 16.2 us
  starting transfers between devices  11 us (67%)
  waiting for transfers between devices  3.17 us (19%)
  Pallas kernels  1.91 us (12%)
    ppermute x7, starting transfers between devices, swap(): return lax.ppermute(x, ('pair', 'virt'), moves)  11 us
    ppermute x7, waiting for transfers between devices, swap(): return lax.ppermute(x, ('pair', 'virt'), moves)  3.17 us
    pallas_call x1, Pallas kernels, prepare(): pl.pallas_call(prepare_kernel, out_shape=[jax.ShapeDtypeStruct(rows_shape...  1.1 us
    pallas_call x1, Pallas kernels, local(): pl.pallas_call(functools.partial(update_kernel, blocks, pair_rows, order,...  0.82 us
  transfers between devices with their start and end apart: 7, of which 2 were waited for; matrix products, arithmetic and copies ran while one was open for 0% of the time, Pallas kernels for 7%

profile of v5, /device:TPU:0, one launch (start us, length us, event | category | flops | bytes accessed | tf_op | source)
XLA Modules:
  0.0 16.2 jit_solution(15401890973772370172)
XLA Ops:
  0.0 4.0 %collective-permute-start = (bf16[1,128,256]{2,1,0:T(8,128)(2,1)}, bf16[1,128,256]{2,1,0:T(8,128)(2,1)S(1)}, u32[]{:S(2)}, u32[]{:S(2)}) collective-permute-start(bf16[1,128,256]{2,1,0:T(8,128)(2,1)} %bitcast.4), channel_id=1, source_target_pairs={{0,16},{1,17},{2,18},{3,19},{4,20},{5,21},{6,22},{7,23},{8,24},{9,... | collective-permute-start | bytes 196616 | tf_op jit(solution)/shard_map/ppermute | solution.py:152
  4.0 2.5 %collective-permute-start.2 = (bf16[1,128,256]{2,1,0:T(8,128)(2,1)}, bf16[1,128,256]{2,1,0:T(8,128)(2,1)S(1)}, u32[]{:S(2)}, u32[]{:S(2)}) collective-permute-start(bf16[1,128,256]{2,1,0:T(8,128)(2,1)} %bitcast.5), channel_id=1, source_target_pairs={{0,12},{1,13},{2,14},{3,15},{4,8},{5,9},{6,10},{7,11},{8,4},{9,5},... | collective-permute-start | bytes 196616 | tf_op jit(solution)/shard_map/ppermute | solution.py:152
  6.5 1.1 %prepare.1 = (bf16[1,4,1024]{2,1,0:T(4,128)(2,1)S(1)}, bf16[1,128,256]{2,1,0:T(8,128)(2,1)S(1)}, f32[16,256]{1,0:T(8,128)S(1)}, f32[16,256]{1,0:T(8,128)S(1)}) custom-call(s32[2,4]{1,0:T(2,128)} %kept_hbm.1, s32[2,2,4]{2,1,0:T(2,128)} %bitcast.6, s32[8]{0:T(128)} %owner_hbm.1, bf16[2,4,2,128]{3,2,1,0:T(2,128)(2,1)} %amp_hbm.1, ...), custom_call_target="tpu_custom_call" | custom-call | tf_op jit(solution)/shard_map/prepare/pallas_call | solution.py:102
  7.6 0.1 collective-permute-start.5
  7.7 0.0 collective-permute-done.refs_3_
  7.8 1.3 %collective-permute-start.1 = (bf16[2,128,256]{2,1,0:T(8,128)(2,1)S(1)}, bf16[2,128,256]{2,1,0:T(8,128)(2,1)S(1)}, u32[]{:S(2)}, u32[]{:S(2)}) collective-permute-start(bf16[2,128,256]{2,1,0:T(8,128)(2,1)S(1)} %constant_dynamic-update-slice_fusion), channel_id=1, source_target_pairs={{0,8},{1,9},{2,10},{3,11},{4,12},{5,13},{6,14},{7,15},{8,0},{9,1},... | collective-permute-start | bytes 393224 | tf_op jit(solution)/shard_map/ppermute | solution.py:152
  9.1 1.1 %collective-permute-start.4 = (bf16[2,128,256]{2,1,0:T(8,128)(2,1)S(1)}, bf16[2,128,256]{2,1,0:T(8,128)(2,1)S(1)}, u32[]{:S(2)}, u32[]{:S(2)}) collective-permute-start(bf16[2,128,256]{2,1,0:T(8,128)(2,1)S(1)} %constant_dynamic-update-slice_fusion), channel_id=1, source_target_pairs={{0,4},{1,5},{2,6},{3,7},{4,0},{5,1},{6,2},{7,3},{8,12},{9,13},{10,... | collective-permute-start | bytes 393224 | tf_op jit(solution)/shard_map/ppermute | solution.py:152
  10.2 1.2 %collective-permute-start.3 = (bf16[1,128,256]{2,1,0:T(8,128)(2,1)S(1)}, bf16[1,128,256]{2,1,0:T(8,128)(2,1)S(1)}, u32[]{:S(2)}, u32[]{:S(2)}) collective-permute-start(bf16[1,128,256]{2,1,0:T(8,128)(2,1)S(1)} %collective-permute-done.refs_3_), channel_id=1, source_target_pairs={{0,12},{1,13},{2,14},{3,15},{4,8},{5,9},{6,10},{7,11},{8,4},{9,5},... | collective-permute-start | bytes 196616 | tf_op jit(solution)/shard_map/ppermute | solution.py:152
  11.3 0.0 collective-permute-done.5
  11.3 0.8 %collective-permute-start.6 = (bf16[2,4,1024]{2,1,0:T(4,128)(2,1)S(1)}, bf16[2,4,1024]{2,1,0:T(4,128)(2,1)S(1)}, u32[]{:S(2)}, u32[]{:S(2)}) collective-permute-start(bf16[2,4,1024]{2,1,0:T(4,128)(2,1)S(1)} %constant_dynamic-update-slice_fusion.2.refs_6_), channel_id=1, source_target_pairs={{0,3},{1,2},{2,1},{3,0},{4,7},{5,6},{6,5},{7,4},{8,11},{9,10},{10,... | collective-permute-start | bytes 49160 | tf_op jit(solution)/shard_map/ppermute | solution.py:152
  12.2 2.5 %collective-permute-done.6.refs_7_ = bf16[2,4,1024]{2,1,0:T(4,128)(2,1)S(1)} collective-permute-done((bf16[2,4,1024]{2,1,0:T(4,128)(2,1)S(1)}, bf16[2,4,1024]{2,1,0:T(4,128)(2,1)S(1)}, u32[]{:S(2)}, u32[]{:S(2)}) %collective-permute-start.6) | collective-permute-done | bytes 16416 | tf_op jit(solution)/shard_map/ppermute | solution.py:152
  14.7 0.0 collective-permute-done.2.refs_2_
  14.7 0.7 %collective-permute-done.3.refs_4_ = bf16[1,128,256]{2,1,0:T(8,128)(2,1)S(1)} collective-permute-done((bf16[1,128,256]{2,1,0:T(8,128)(2,1)S(1)}, bf16[1,128,256]{2,1,0:T(8,128)(2,1)S(1)}, u32[]{:S(2)}, u32[]{:S(2)}) %collective-permute-start.3) | collective-permute-done | bytes 65568 | tf_op jit(solution)/shard_map/ppermute | solution.py:152
  15.3 0.0 collective-permute-done.1.refs_0_
  15.3 0.0 collective-permute-done.4.refs_5_
  15.3 0.8 %update.1 = f32[16,256]{1,0:T(8,128)} custom-call(bf16[2,128,256]{2,1,0:T(8,128)(2,1)S(1)} %collective-permute-done.1.refs_0_, bf16[1,128,256]{2,1,0:T(8,128)(2,1)S(1)} %get-tuple-element.9.refs_1_, bf16[1,128,256]{2,1,0:T(8,128)(2,1)S(1)} %collective-permute-done.2.refs_2_, bf16[1,128,256]{2,1,0:T(8,128)(2,1)S(1)} %collective-permute-done.refs_3_, ...), custom_call_target="tpu_custom_call" | custom-call | tf_op jit(solution)/shard_map/update/pallas_call | solution.py:188
  (4 shorter events, 0.0 us)
Async XLA Ops:
  0.0 7.7 %collective-permute-start = (bf16[1,128,256]{2,1,0:T(8,128)(2,1)}, bf16[1,128,256]{2,1,0:T(8,128)(2,1)S(1)}, u32[]{:S(2)}, u32[]{:S(2)}) collective-permute-start(bf16[1,128,256]{2,1,0:T(8,128)(2,1)} %bitcast.4), channel_id=1, source_target_pairs={{0,16},{1,17},{2,18},{3,19},{4,20},{5,21},{6,22},{7,23},{8,24},{9,... | collective-permute-start | bytes 196616 | tf_op jit(solution)/shard_map/ppermute | solution.py:152
  4.0 10.6 %collective-permute-start.2 = (bf16[1,128,256]{2,1,0:T(8,128)(2,1)}, bf16[1,128,256]{2,1,0:T(8,128)(2,1)S(1)}, u32[]{:S(2)}, u32[]{:S(2)}) collective-permute-start(bf16[1,128,256]{2,1,0:T(8,128)(2,1)} %bitcast.5), channel_id=1, source_target_pairs={{0,12},{1,13},{2,14},{3,15},{4,8},{5,9},{6,10},{7,11},{8,4},{9,5},... | collective-permute-start | bytes 196616 | tf_op jit(solution)/shard_map/ppermute | solution.py:152
  7.6 3.7 %collective-permute-start.5 = (bf16[1,4,1024]{2,1,0:T(4,128)(2,1)S(1)}, bf16[1,4,1024]{2,1,0:T(4,128)(2,1)S(1)}, u32[]{:S(2)}, u32[]{:S(2)}) collective-permute-start(bf16[1,4,1024]{2,1,0:T(4,128)(2,1)S(1)} %get-tuple-element.10), channel_id=1, source_target_pairs={{0,1},{1,0},{2,3},{3,2},{4,5},{5,4},{6,7},{7,6},{8,9},{9,8},{10,11... | collective-permute-start | bytes 24584 | tf_op jit(solution)/shard_map/ppermute | solution.py:152
  7.8 7.6 %collective-permute-start.1 = (bf16[2,128,256]{2,1,0:T(8,128)(2,1)S(1)}, bf16[2,128,256]{2,1,0:T(8,128)(2,1)S(1)}, u32[]{:S(2)}, u32[]{:S(2)}) collective-permute-start(bf16[2,128,256]{2,1,0:T(8,128)(2,1)S(1)} %constant_dynamic-update-slice_fusion), channel_id=1, source_target_pairs={{0,8},{1,9},{2,10},{3,11},{4,12},{5,13},{6,14},{7,15},{8,0},{9,1},... | collective-permute-start | bytes 393224 | tf_op jit(solution)/shard_map/ppermute | solution.py:152
  9.1 6.3 %collective-permute-start.4 = (bf16[2,128,256]{2,1,0:T(8,128)(2,1)S(1)}, bf16[2,128,256]{2,1,0:T(8,128)(2,1)S(1)}, u32[]{:S(2)}, u32[]{:S(2)}) collective-permute-start(bf16[2,128,256]{2,1,0:T(8,128)(2,1)S(1)} %constant_dynamic-update-slice_fusion), channel_id=1, source_target_pairs={{0,4},{1,5},{2,6},{3,7},{4,0},{5,1},{6,2},{7,3},{8,12},{9,13},{10,... | collective-permute-start | bytes 393224 | tf_op jit(solution)/shard_map/ppermute | solution.py:152
  10.2 5.2 %collective-permute-start.3 = (bf16[1,128,256]{2,1,0:T(8,128)(2,1)S(1)}, bf16[1,128,256]{2,1,0:T(8,128)(2,1)S(1)}, u32[]{:S(2)}, u32[]{:S(2)}) collective-permute-start(bf16[1,128,256]{2,1,0:T(8,128)(2,1)S(1)} %collective-permute-done.refs_3_), channel_id=1, source_target_pairs={{0,12},{1,13},{2,14},{3,15},{4,8},{5,9},{6,10},{7,11},{8,4},{9,5},... | collective-permute-start | bytes 196616 | tf_op jit(solution)/shard_map/ppermute | solution.py:152
  11.3 3.3 %collective-permute-start.6 = (bf16[2,4,1024]{2,1,0:T(4,128)(2,1)S(1)}, bf16[2,4,1024]{2,1,0:T(4,128)(2,1)S(1)}, u32[]{:S(2)}, u32[]{:S(2)}) collective-permute-start(bf16[2,4,1024]{2,1,0:T(4,128)(2,1)S(1)} %constant_dynamic-update-slice_fusion.2.refs_6_), channel_id=1, source_target_pairs={{0,3},{1,2},{2,1},{3,0},{4,7},{5,6},{6,5},{7,4},{8,11},{9,10},{10,... | collective-permute-start | bytes 49160 | tf_op jit(solution)/shard_map/ppermute | solution.py:152

commit v6 on v5

--- a/solution.py
+++ b/solution.py
@@ -181,10 +181,10 @@
         order = order + [at ^ mask for at in order]
 
     both = jnp.concatenate([own, far], axis=0)
-    along_x = swap(both, 1, 0)
     beyond = swap(far, 3, 0)
     along_z = swap(both, 2, 0)
-    arrays = [(along_z, (2, 6)), (own, (0,)), (diagonal, (3,)), (far, (4,)), (beyond, (7,)), (along_x, (1, 5))]
+    along_x = swap(both, 1, 0)
+    arrays = [(far, (4,)), (beyond, (7,)), (along_z, (2, 6)), (own, (0,)), (along_x, (1, 5)), (diagonal, (3,))]
     return pl.pallas_call(
         functools.partial(update_kernel, blocks, pair_rows, order, [at for _, at in arrays]),
         out_shape=jax.ShapeDtypeStruct(residual_in.shape, jnp.float32),

time: 16.3 us -> 16.3 us (level)
  no operation moved by 1% of the time
where the time goes in v6:
time: 16.3 us; the launch traced here: 16.2 us
  starting transfers between devices  11 us (67%)
  waiting for transfers between devices  3.17 us (19%)
  Pallas kernels  1.91 us (12%)
    ppermute x7, starting transfers between devices, swap(): return lax.ppermute(x, ('pair', 'virt'), moves)  11 us
    ppermute x7, waiting for transfers between devices, swap(): return lax.ppermute(x, ('pair', 'virt'), moves)  3.17 us
    pallas_call x1, Pallas kernels, prepare(): pl.pallas_call(prepare_kernel, out_shape=[jax.ShapeDtypeStruct(rows_shape...  1.1 us
    pallas_call x1, Pallas kernels, local(): pl.pallas_call(functools.partial(update_kernel, blocks, pair_rows, order,...  0.81 us
  transfers between devices with their start and end apart: 7, of which 2 were waited for; matrix products, arithmetic and copies ran while one was open for 0% of the time, Pallas kernels for 7%

profile of v6, /device:TPU:0, one launch (start us, length us, event | category | flops | bytes accessed | tf_op | source)
XLA Modules:
  0.0 16.2 jit_solution(13378746367939621744)
XLA Ops:
  0.0 4.0 %collective-permute-start = (bf16[1,128,256]{2,1,0:T(8,128)(2,1)}, bf16[1,128,256]{2,1,0:T(8,128)(2,1)S(1)}, u32[]{:S(2)}, u32[]{:S(2)}) collective-permute-start(bf16[1,128,256]{2,1,0:T(8,128)(2,1)} %bitcast.4), channel_id=1, source_target_pairs={{0,16},{1,17},{2,18},{3,19},{4,20},{5,21},{6,22},{7,23},{8,24},{9,... | collective-permute-start | bytes 196616 | tf_op jit(solution)/shard_map/ppermute | solution.py:152
  4.0 2.5 %collective-permute-start.4 = (bf16[1,128,256]{2,1,0:T(8,128)(2,1)}, bf16[1,128,256]{2,1,0:T(8,128)(2,1)S(1)}, u32[]{:S(2)}, u32[]{:S(2)}) collective-permute-start(bf16[1,128,256]{2,1,0:T(8,128)(2,1)} %bitcast.5), channel_id=1, source_target_pairs={{0,12},{1,13},{2,14},{3,15},{4,8},{5,9},{6,10},{7,11},{8,4},{9,5},... | collective-permute-start | bytes 196616 | tf_op jit(solution)/shard_map/ppermute | solution.py:152
  6.5 1.1 %prepare.1 = (bf16[1,4,1024]{2,1,0:T(4,128)(2,1)S(1)}, bf16[1,128,256]{2,1,0:T(8,128)(2,1)S(1)}, f32[16,256]{1,0:T(8,128)S(1)}, f32[16,256]{1,0:T(8,128)S(1)}) custom-call(s32[2,4]{1,0:T(2,128)} %kept_hbm.1, s32[2,2,4]{2,1,0:T(2,128)} %bitcast.6, s32[8]{0:T(128)} %owner_hbm.1, bf16[2,4,2,128]{3,2,1,0:T(2,128)(2,1)} %amp_hbm.1, ...), custom_call_target="tpu_custom_call" | custom-call | tf_op jit(solution)/shard_map/prepare/pallas_call | solution.py:102
  7.6 0.1 collective-permute-start.5
  7.7 0.0 collective-permute-done.refs_0_
  7.8 1.3 %collective-permute-start.2 = (bf16[2,128,256]{2,1,0:T(8,128)(2,1)S(1)}, bf16[2,128,256]{2,1,0:T(8,128)(2,1)S(1)}, u32[]{:S(2)}, u32[]{:S(2)}) collective-permute-start(bf16[2,128,256]{2,1,0:T(8,128)(2,1)S(1)} %constant_dynamic-update-slice_fusion), channel_id=1, source_target_pairs={{0,8},{1,9},{2,10},{3,11},{4,12},{5,13},{6,14},{7,15},{8,0},{9,1},... | collective-permute-start | bytes 393224 | tf_op jit(solution)/shard_map/ppermute | solution.py:152
  9.1 1.1 %collective-permute-start.3 = (bf16[2,128,256]{2,1,0:T(8,128)(2,1)S(1)}, bf16[2,128,256]{2,1,0:T(8,128)(2,1)S(1)}, u32[]{:S(2)}, u32[]{:S(2)}) collective-permute-start(bf16[2,128,256]{2,1,0:T(8,128)(2,1)S(1)} %constant_dynamic-update-slice_fusion), channel_id=1, source_target_pairs={{0,4},{1,5},{2,6},{3,7},{4,0},{5,1},{6,2},{7,3},{8,12},{9,13},{10,... | collective-permute-start | bytes 393224 | tf_op jit(solution)/shard_map/ppermute | solution.py:152
  10.2 1.2 %collective-permute-start.1 = (bf16[1,128,256]{2,1,0:T(8,128)(2,1)S(1)}, bf16[1,128,256]{2,1,0:T(8,128)(2,1)S(1)}, u32[]{:S(2)}, u32[]{:S(2)}) collective-permute-start(bf16[1,128,256]{2,1,0:T(8,128)(2,1)S(1)} %collective-permute-done.refs_0_), channel_id=1, source_target_pairs={{0,12},{1,13},{2,14},{3,15},{4,8},{5,9},{6,10},{7,11},{8,4},{9,5},... | collective-permute-start | bytes 196616 | tf_op jit(solution)/shard_map/ppermute | solution.py:152
  11.3 0.0 collective-permute-done.5
  11.3 0.8 %collective-permute-start.6 = (bf16[2,4,1024]{2,1,0:T(4,128)(2,1)S(1)}, bf16[2,4,1024]{2,1,0:T(4,128)(2,1)S(1)}, u32[]{:S(2)}, u32[]{:S(2)}) collective-permute-start(bf16[2,4,1024]{2,1,0:T(4,128)(2,1)S(1)} %constant_dynamic-update-slice_fusion.2.refs_6_), channel_id=1, source_target_pairs={{0,3},{1,2},{2,1},{3,0},{4,7},{5,6},{6,5},{7,4},{8,11},{9,10},{10,... | collective-permute-start | bytes 49160 | tf_op jit(solution)/shard_map/ppermute | solution.py:152
  12.2 2.5 %collective-permute-done.6.refs_7_ = bf16[2,4,1024]{2,1,0:T(4,128)(2,1)S(1)} collective-permute-done((bf16[2,4,1024]{2,1,0:T(4,128)(2,1)S(1)}, bf16[2,4,1024]{2,1,0:T(4,128)(2,1)S(1)}, u32[]{:S(2)}, u32[]{:S(2)}) %collective-permute-start.6) | collective-permute-done | bytes 16416 | tf_op jit(solution)/shard_map/ppermute | solution.py:152
  14.7 0.0 collective-permute-done.4.refs_5_
  14.7 0.7 %collective-permute-done.1.refs_1_ = bf16[1,128,256]{2,1,0:T(8,128)(2,1)S(1)} collective-permute-done((bf16[1,128,256]{2,1,0:T(8,128)(2,1)S(1)}, bf16[1,128,256]{2,1,0:T(8,128)(2,1)S(1)}, u32[]{:S(2)}, u32[]{:S(2)}) %collective-permute-start.1) | collective-permute-done | bytes 65568 | tf_op jit(solution)/shard_map/ppermute | solution.py:152
  15.3 0.0 collective-permute-done.2.refs_2_
  15.3 0.0 collective-permute-done.3.refs_4_
  15.3 0.8 %update.1 = f32[16,256]{1,0:T(8,128)} custom-call(bf16[1,128,256]{2,1,0:T(8,128)(2,1)S(1)} %collective-permute-done.refs_0_, bf16[1,128,256]{2,1,0:T(8,128)(2,1)S(1)} %collective-permute-done.1.refs_1_, bf16[2,128,256]{2,1,0:T(8,128)(2,1)S(1)} %collective-permute-done.2.refs_2_, bf16[1,128,256]{2,1,0:T(8,128)(2,1)S(1)} %get-tuple-element.9.refs_3_, ...), custom_call_target="tpu_custom_call" | custom-call | tf_op jit(solution)/shard_map/update/pallas_call | solution.py:188
  (4 shorter events, 0.0 us)
Async XLA Ops:
  0.0 7.7 %collective-permute-start = (bf16[1,128,256]{2,1,0:T(8,128)(2,1)}, bf16[1,128,256]{2,1,0:T(8,128)(2,1)S(1)}, u32[]{:S(2)}, u32[]{:S(2)}) collective-permute-start(bf16[1,128,256]{2,1,0:T(8,128)(2,1)} %bitcast.4), channel_id=1, source_target_pairs={{0,16},{1,17},{2,18},{3,19},{4,20},{5,21},{6,22},{7,23},{8,24},{9,... | collective-permute-start | bytes 196616 | tf_op jit(solution)/shard_map/ppermute | solution.py:152
  4.0 10.6 %collective-permute-start.4 = (bf16[1,128,256]{2,1,0:T(8,128)(2,1)}, bf16[1,128,256]{2,1,0:T(8,128)(2,1)S(1)}, u32[]{:S(2)}, u32[]{:S(2)}) collective-permute-start(bf16[1,128,256]{2,1,0:T(8,128)(2,1)} %bitcast.5), channel_id=1, source_target_pairs={{0,12},{1,13},{2,14},{3,15},{4,8},{5,9},{6,10},{7,11},{8,4},{9,5},... | collective-permute-start | bytes 196616 | tf_op jit(solution)/shard_map/ppermute | solution.py:152
  7.6 3.7 %collective-permute-start.5 = (bf16[1,4,1024]{2,1,0:T(4,128)(2,1)S(1)}, bf16[1,4,1024]{2,1,0:T(4,128)(2,1)S(1)}, u32[]{:S(2)}, u32[]{:S(2)}) collective-permute-start(bf16[1,4,1024]{2,1,0:T(4,128)(2,1)S(1)} %get-tuple-element.10), channel_id=1, source_target_pairs={{0,1},{1,0},{2,3},{3,2},{4,5},{5,4},{6,7},{7,6},{8,9},{9,8},{10,11... | collective-permute-start | bytes 24584 | tf_op jit(solution)/shard_map/ppermute | solution.py:152
  7.8 7.6 %collective-permute-start.2 = (bf16[2,128,256]{2,1,0:T(8,128)(2,1)S(1)}, bf16[2,128,256]{2,1,0:T(8,128)(2,1)S(1)}, u32[]{:S(2)}, u32[]{:S(2)}) collective-permute-start(bf16[2,128,256]{2,1,0:T(8,128)(2,1)S(1)} %constant_dynamic-update-slice_fusion), channel_id=1, source_target_pairs={{0,8},{1,9},{2,10},{3,11},{4,12},{5,13},{6,14},{7,15},{8,0},{9,1},... | collective-permute-start | bytes 393224 | tf_op jit(solution)/shard_map/ppermute | solution.py:152
  9.1 6.3 %collective-permute-start.3 = (bf16[2,128,256]{2,1,0:T(8,128)(2,1)S(1)}, bf16[2,128,256]{2,1,0:T(8,128)(2,1)S(1)}, u32[]{:S(2)}, u32[]{:S(2)}) collective-permute-start(bf16[2,128,256]{2,1,0:T(8,128)(2,1)S(1)} %constant_dynamic-update-slice_fusion), channel_id=1, source_target_pairs={{0,4},{1,5},{2,6},{3,7},{4,0},{5,1},{6,2},{7,3},{8,12},{9,13},{10,... | collective-permute-start | bytes 393224 | tf_op jit(solution)/shard_map/ppermute | solution.py:152
  10.2 5.2 %collective-permute-start.1 = (bf16[1,128,256]{2,1,0:T(8,128)(2,1)S(1)}, bf16[1,128,256]{2,1,0:T(8,128)(2,1)S(1)}, u32[]{:S(2)}, u32[]{:S(2)}) collective-permute-start(bf16[1,128,256]{2,1,0:T(8,128)(2,1)S(1)} %collective-permute-done.refs_0_), channel_id=1, source_target_pairs={{0,12},{1,13},{2,14},{3,15},{4,8},{5,9},{6,10},{7,11},{8,4},{9,5},... | collective-permute-start | bytes 196616 | tf_op jit(solution)/shard_map/ppermute | solution.py:152
  11.3 3.3 %collective-permute-start.6 = (bf16[2,4,1024]{2,1,0:T(4,128)(2,1)S(1)}, bf16[2,4,1024]{2,1,0:T(4,128)(2,1)S(1)}, u32[]{:S(2)}, u32[]{:S(2)}) collective-permute-start(bf16[2,4,1024]{2,1,0:T(4,128)(2,1)S(1)} %constant_dynamic-update-slice_fusion.2.refs_6_), channel_id=1, source_target_pairs={{0,3},{1,2},{2,1},{3,0},{4,7},{5,6},{6,5},{7,4},{8,11},{9,10},{10,... | collective-permute-start | bytes 49160 | tf_op jit(solution)/shard_map/ppermute | solution.py:152
